TPU v7x, 512 devices: a whole 4x4x16 slice. The times are simulated.
512 devices in a mesh: ctx: 64 (over z, y), head: 8 (over x, core).
Axes of the slice: x: 4, y: 4, z: 16, core: 2. Of those that a mesh axis runs over, the one named last changes fastest.
Arguments:
- queries: bfloat16 [16384, 4096], P('ctx', 'head'), may hold values from -6 to 6
- keys: bfloat16 [16384, 4096], P('ctx', 'head'), may hold values from -6 to 6
- values: bfloat16 [16384, 4096], P('ctx', 'head'), may hold values from -6 to 6
- out_grad: bfloat16 [16384, 4096], P('ctx', 'head'), may hold values from -6 to 6
- out_weight: bfloat16 [16, 256, 4096], P('head', 'ctx'), may hold values from -0.09375 to 0.09375
- decay_rate: float32 [16], P('head'), may hold values from 0.00024414062 to 0.025
- doc_spans: int32 [21], replicated, may hold values from 1 to 4, 64 in all
Outputs:
- query_grad: bfloat16 [16384, 4096], P('ctx', 'head')
- key_grad: bfloat16 [16384, 4096], P('ctx', 'head')
- value_grad: bfloat16 [16384, 4096], P('ctx', 'head')
Inputs may be any that keep to these rules, and one draw needn't show every extreme that they name: `doc_spans`: each length counts whole spans of 256 tokens; the lengths sum to 64 and the longest is exactly 4.
All inputs are finite; a program needn't handle non-finite values.
Results may differ from a plain program's by a relative error of at most 0.007.
Values may be sent and summed in bfloat16 or wider, within the bound.
No kernel may reach another device: no remote copies, remote signals or barrier semaphores. Data moves between devices by JAX's collectives and lax.ppermute only.
A program may use at most 128 MiB of HBM per device.

v0:
```python
import jax
import jax.numpy as jnp
from jax import lax
from jax.sharding import PartitionSpec as P

DK = 256
DV = 256
SPAN = 256


EPS = 1e-05
PREC = lax.Precision.HIGHEST


def carried_in(shard, axis, combine, identity, reverse):
    length, place = (lax.axis_size(axis), lax.axis_index(axis))
    everything = jax.tree.map(lambda part: lax.all_gather(part, axis), shard)
    start = jax.tree.map(
        lambda part, zero: jnp.broadcast_to(jnp.asarray(zero, part.dtype), part.shape),
        shard,
        identity,
    )

    def hop(k, before):
        at = length - 1 - k if reverse else k
        reached = at > place if reverse else at < place
        new = combine(before, jax.tree.map(lambda part: part[at], everything))
        return jax.tree.map(lambda a, b: jnp.where(reached, a, b), new, before)

    return lax.fori_loop(0, length, hop, start)


def decay_tables(decay_rate):
    offset = jnp.arange(SPAN, dtype=jnp.float32)
    distance = offset[:, None] - offset[None, :]
    decay_mask = jnp.where(
        distance[None] >= 0.0,
        jnp.exp(-decay_rate[:, None, None] * jnp.maximum(distance, 0.0)[None]),
        0.0,
    )
    query_decay = jnp.exp(-decay_rate[:, None] * offset[None, :]).T
    key_decay = jnp.exp(-decay_rate[:, None] * (SPAN - offset)[None, :]).T
    whole_decay = jnp.exp(-decay_rate * SPAN)
    return (decay_mask, query_decay, key_decay, whole_decay)


def group_norm(output):
    centred = output - jnp.mean(output, axis=-1, keepdims=True)
    variance = jnp.mean(centred * centred, axis=-1, keepdims=True)
    return centred * lax.rsqrt(variance + EPS)


def join(earlier, later):
    return (earlier[0] * later[0], later[0][:, None, None] * earlier[1] + later[1])


def shards(queries, keys, values, out_grad, out_weight, decay_rate, doc_spans):
    heads = decay_rate.shape[0]
    rows = queries.shape[0]
    count = rows // SPAN
    scale = DK ** (-0.5)
    decay_mask, query_decay, key_decay, whole_decay = decay_tables(decay_rate)
    total_spans = count * lax.axis_size("ctx")
    firsts = jnp.cumsum(doc_spans) - doc_spans
    all_starts = jnp.any(
        jnp.arange(total_spans, dtype=jnp.int32)[:, None] == firsts[None, :], axis=1
    )
    offset_span = lax.axis_index("ctx") * count
    starts = lax.dynamic_slice_in_dim(all_starts, offset_span, count, 0)
    first_start = starts[0]
    inner_start = jnp.any(starts[1:])
    block_decay = jnp.where(first_start | inner_start, 0.0, jnp.exp(-decay_rate * rows))
    identity = (jnp.ones((heads,), jnp.float32), jnp.zeros((heads, DK, DV), jnp.float32))
    q_all = queries.reshape(count, SPAN, heads, DK)
    k_all = keys.reshape(count, SPAN, heads, DK)
    v_all = values.reshape(count, SPAN, heads, DV)
    number = 0
    k_scaled = k_all[number].astype(jnp.float32) * key_decay[:, :, None]
    updates = [
        jnp.einsum("shd,she->hde", k_scaled, v_all[number].astype(jnp.float32), precision=PREC)
    ]
    local_state = jnp.zeros((heads, DK, DV), jnp.float32)
    number = 0
    local_state = whole_decay[:, None, None] * local_state + updates[number]
    element = (block_decay, local_state)
    arrived = carried_in(element, "ctx", join, identity, False)[1]
    state = jnp.where(first_start, 0.0, arrived)
    number = 0
    states_in = [state]
    raw = jnp.einsum(
        "thd,shd->hts", q_all[number], k_all[number], preferred_element_type=jnp.float32
    )
    weights = (raw * scale * decay_mask).astype(jnp.bfloat16)
    weight_blocks = [weights]
    output = jnp.einsum("hts,she->the", weights, v_all[number], preferred_element_type=jnp.float32)
    q_float = q_all[number].astype(jnp.float32)
    output = output + scale * query_decay[:, :, None] * jnp.einsum(
        "thd,hde->the", q_float, state, precision=PREC
    )
    features_all = lax.all_gather(out_grad, "head", axis=1, tiled=True)
    norm_grad = lax.dot_general(
        features_all,
        lax.all_gather(out_weight, "ctx", axis=1, tiled=True),
        (((1,), (2,)), ((), ())),
        preferred_element_type=jnp.float32,
    )
    _, pullback = jax.vjp(group_norm, output)
    retained_grad = pullback(norm_grad)[0]
    g_all = retained_grad.reshape(count, SPAN, heads, DV)
    number = 0
    q_scaled = q_all[number].astype(jnp.float32) * query_decay[:, :, None]
    sources = [jnp.einsum("thd,the->hde", q_scaled, g_all[number], precision=PREC)]
    local_total = jnp.zeros((heads, DK, DV), jnp.float32)
    for number in reversed(range(count)):
        local_total = whole_decay[:, None, None] * local_total + sources[number]
    back_element = (block_decay, jnp.where(first_start, 0.0, local_total))
    later = carried_in(back_element, "ctx", join, identity, True)[1]
    q_grads = [None] * count
    k_grads = [None] * count
    v_grads = [None] * count
    for number in reversed(range(count)):
        q_block = q_all[number]
        k_block = k_all[number]
        v_block = v_all[number]
        g_block = g_all[number]
        g_round = g_block.astype(jnp.bfloat16)
        raw_grad = (
            jnp.einsum("the,she->hts", g_round, v_block, preferred_element_type=jnp.float32)
            * decay_mask
        )
        dscores = raw_grad.astype(jnp.bfloat16)
        q_grad = jnp.einsum("hts,shd->thd", dscores, k_block, preferred_element_type=jnp.float32)
        q_grad = q_grad + query_decay[:, :, None] * jnp.einsum(
            "hde,the->thd", states_in[number], g_block, precision=PREC
        )
        k_grad = jnp.einsum("hts,thd->shd", dscores, q_block, preferred_element_type=jnp.float32)
        k_grad = k_grad + key_decay[:, :, None] * jnp.einsum(
            "hde,she->shd", later, v_block.astype(jnp.float32), precision=PREC
        )
        v_grad = jnp.einsum(
            "hts,the->she", weight_blocks[number], g_round, preferred_element_type=jnp.float32
        )
        v_grad = v_grad + scale * key_decay[:, :, None] * jnp.einsum(
            "hde,shd->she", later, k_block.astype(jnp.float32), precision=PREC
        )
        q_grads[number] = scale * q_grad
        k_grads[number] = scale * k_grad
        v_grads[number] = v_grad
    query_grad = q_grads[0].reshape(rows, heads * DK).astype(jnp.bfloat16)
    key_grad = k_grads[0].reshape(rows, heads * DK).astype(jnp.bfloat16)
    value_grad = v_grads[0].reshape(rows, heads * DV).astype(jnp.bfloat16)
    return (query_grad, key_grad, value_grad)


def solution(mesh):
    in_specs = (
        P("ctx", "head"),
        P("ctx", "head"),
        P("ctx", "head"),
        P("ctx", "head"),
        P("head", "ctx", None),
        P("head"),
        P(),
    )
    out_specs = (P("ctx", "head"), P("ctx", "head"), P("ctx", "head"))
    return jax.shard_map(shards, mesh=mesh, in_specs=in_specs, out_specs=out_specs, check_vma=False)
```

profile of v0, /device:TPU:1, one launch (start us, length us, event | category | flops | bytes accessed | tf_op | source)
XLA Modules:
  0.0 885.2 jit_solution(4287778965514714641)
XLA Ops:
  10.0 1.3 dynamic-slice
  12.5 1.4 broadcast_multiply_fusion.3
  14.0 2.2 convolution_add_fusion.1
  17.0 1.5 copy.69
  18.8 123.6 %all-reduce = f32[128]{0:T(128)S(1)} all-reduce(f32[128]{0:T(128)S(1)} %get-tuple-element.310), channel_id=2, replica_groups=mesh['ctx'=64,'head'=8] {'ctx'}, use_global_device_ids=true, to_apply=%add | all-reduce | flops 128 | bytes 1024
  143.9 172.5 %all-gather.12.cloned.1.call-done = f32[128,256,256]{2,1,0:T(8,128)} async-done(((f32[2,256,256]{2,1,0:T(8,128)}), f32[128,256,256]{2,1,0:T(8,128)}) %all-gather.12.cloned.1.call-update) | async-done | bytes 33554448 | tf_op jit(solution)/shard_map/all_gather | solution.py:17
  316.3 77.9 %while.30 = (s32[]{:T(128)}, f32[2,256,256]{2,1,0:T(8,128)S(1)}, s32[]{:T(128)}, f32[64,2]{1,0:T(8,128)S(1)}, f32[64,2,256,256]{3,2,1,0:T(8,128)}, /*index=5*/s32[]{:T(128)}, s32[]{:T(128)}) while((s32[]{:T(128)}, f32[2,256,256]{2,1,0:T(8,128)S(1)}, s32[]{:T(128)}, f32[64,2]{1,0:T(8,128)S(1)}, f32[64,2,256,256]{3,2,1,0:T(8,128)}, ...), condition=%wide.region_3.4_spmd.clone, body=%wide.region_2.3_spmd.clone.sunk | while | flops 524292 | bytes 1573001 | solution.py:30
  316.3 1.2 fusion.69
  331.0 1.2 fusion.69
  332.2 1.2 fusion.69
  337.1 1.2 fusion.69
  338.3 1.2 fusion.69
  339.5 1.2 fusion.69
  340.7 1.2 fusion.69
  373.6 1.2 fusion.69
  389.4 1.2 fusion.69
  391.8 1.2 fusion.69
  394.2 1.3 fusion.14
  395.9 94.5 %all-gather.10.cloned.1.call-done = bf16[2,256,4096]{2,0,1:T(2,128)(2,1)} async-done(((bf16[2,4,4096]{2,0,1:T(2,128)(2,1)}), bf16[2,256,4096]{2,0,1:T(2,128)(2,1)}) %all-gather.10.cloned.1.call-update) | async-done | bytes 4194320 | tf_op jit(solution)/shard_map/all_gather | solution.py:103
  490.4 7.6 multiply_reduce_fusion.1
  498.1 2.2 fusion.5
  500.6 1.3 fusion.12
  503.0 294.1 %all-gather.14.cloned.1.call-done = f32[128,256,256]{2,1,0:T(8,128)} async-done(((f32[2,256,256]{2,1,0:T(8,128)}), f32[128,256,256]{2,1,0:T(8,128)}) %all-gather.14.cloned.1.call-update) | async-done | bytes 33554448 | tf_op jit(solution)/shard_map/all_gather | solution.py:17
  797.2 78.3 %while.31 = (s32[]{:T(128)}, f32[2,256,256]{2,1,0:T(8,128)S(1)}, s32[]{:T(128)}, f32[64,2]{1,0:T(8,128)S(1)}, f32[64,2,256,256]{3,2,1,0:T(8,128)}, /*index=5*/s32[]{:T(128)}, s32[]{:T(128)}, s32[]{:T(128)}, s32[]{:T(128)}) while((s32[]{:T(128)}, f32[2,256,256]{2,1,0:T(8,128)S(1)}, s32[]{:T(128)}, f32[64,2]{1,0:T(8,128)S(1)}, ...), condition=%wide.region_9.10_spmd.clone, body=%wide.region_8.9_spmd.clone.sunk | while | flops 524296 | bytes 1573063 | solution.py:30
  (288 shorter events, 150.6 us)
Async XLA Ops:
  7.2 309.2 %all-gather.12.cloned.1.call-start = ((), (), s32[]{:S(2)}) async-start(), calls=%async_computation.2 | async-start | bytes 34078720 | tf_op jit(solution)/shard_map/all_gather | solution.py:17
  16.2 379.7 %all-gather.8.cloned.1.call-start = ((), (), s32[]{:S(2)}) async-start(), calls=%async_computation | async-start | bytes 2359296 | tf_op jit(solution)/shard_map/all_gather | solution.py:100
  16.9 473.4 %all-gather.10.cloned.1.call-start = ((), (), s32[]{:S(2)}) async-start(), calls=%async_computation.1 | async-start | bytes 4259840 | tf_op jit(solution)/shard_map/all_gather | solution.py:103
  18.5 778.6 %all-gather.14.cloned.1.call-start = ((), (), s32[]{:S(2)}) async-start(), calls=%async_computation.3 | async-start | bytes 34078720 | tf_op jit(solution)/shard_map/all_gather | solution.py:17
  316.3 79.2 %copy-start = (bf16[256,512]{1,0:T(8,128)(2,1)S(1)}, bf16[256,512]{1,0:T(8,128)(2,1)}, u32[]{:S(2)}) copy-start(bf16[256,512]{1,0:T(8,128)(2,1)} %param.13) | copy-start | bytes 786436
Sparse Core Ops, SparseCore 0:
  16.3 299.9 all-gather.11
  318.5 29.9 all-gather.7
  352.0 138.3 all-gather.9
  500.4 296.7 all-gather.13
where the time goes:
time: 892 us; the launch traced here: 885 us
  waiting for transfers between devices  562 us (63%)
  other arithmetic  153 us (17%)
  blocking collectives  124 us (14%)
  matrix products  17.2 us (2%)
  between operations  14.6 us (2%)
  local copies, waits for them, and re-layouts  10.2 us (1%)
    all_gather x2, waiting for transfers between devices, carried_in(): everything = jax.tree.map(lambda part: lax.all_gather(part, axis), shard)  467 us
    select_n x128, other arithmetic, hop(): return jax.tree.map(lambda a, b: jnp.where(reached, a, b), new, before)  150 us
    unnamed x1, blocking collectives  124 us
    all_gather x1, waiting for transfers between devices, shards(): lax.all_gather(out_weight, 'ctx', axis=1, tiled=True)  94.5 us
  transfers between devices with their start and end apart: 4, of which 3 were waited for; matrix products, arithmetic and copies ran while one was open for 9% of the time, Pallas kernels for 0%

commit v1 on v0

v1 whole, which is shorter than its diff:
```python
import jax
import jax.numpy as jnp
from jax import lax
from jax.experimental import pallas as pl
from jax.experimental.pallas import tpu as pltpu
from jax.sharding import Mesh, PartitionSpec as P

DK = 256
DV = 256
SPAN = 256
HEADS = 2
REACH = 3
EPS = 1e-05
SCALE = DK**-0.5
F32 = jnp.float32
BF16 = jnp.bfloat16
PREC = lax.Precision.HIGHEST
NEAR = (0, 1, -1, 2)
LOW = 32
SENT = SPAN + LOW

Z1, Z0, Y, X, CORE = 4, 4, 4, 4, 2
Z = Z1 * Z0
DEPTH = ("z1", "z0")
CTX = ("z1", "z0", "y")
HEAD = ("x", "core")

SMEM = pl.BlockSpec(memory_space=pltpu.SMEM)
VMEM = pl.BlockSpec(memory_space=pltpu.VMEM)
HBM = pl.BlockSpec(memory_space=pltpu.HBM)
ANY = pl.BlockSpec(memory_space=pl.ANY)


def dot(a, b, dims, precision=None):
    return lax.dot_general(a, b, ((dims[:1], dims[1:]), ((), ())), precision=precision, preferred_element_type=F32)


def nn(a, b, precision=None):
    return dot(a, b, (1, 0), precision)


def nt(a, b, precision=None):
    return dot(a, b, (1, 1), precision)


def tn(a, b, precision=None):
    return dot(a, b, (0, 0), precision)


def cols(h):
    return slice(h * 256, (h + 1) * 256)


def offsets():
    return lax.broadcasted_iota(jnp.int32, (SPAN, 1), 0).astype(F32)


def decay_mask(rate):
    t = lax.broadcasted_iota(jnp.int32, (SPAN, SPAN), 0)
    s = lax.broadcasted_iota(jnp.int32, (SPAN, SPAN), 1)
    distance = jnp.maximum(t - s, 0).astype(F32)
    return jnp.where(t >= s, jnp.exp(-rate * distance), 0.0)


def joined(spans_ref, towards):
    place = (lax.axis_index("z1") * Z0 + lax.axis_index("z0")) * Y + lax.axis_index("y")
    edges = [place + 1 + j if towards > 0 else place - j for j in range(REACH)]
    cut = [jnp.int32(0)] * REACH
    first = jnp.int32(0)
    for i in range(spans_ref.shape[0] + 1):
        cut = [c + (first == e).astype(jnp.int32) for c, e in zip(cut, edges)]
        if i < spans_ref.shape[0]:
            first = first + spans_ref[i]
    out, total = [], jnp.int32(0)
    for c in cut:
        total = total + c
        out.append(jnp.where(total == 0, 1.0, 0.0).astype(F32))
    return out


def combined(states, links, rate, h):
    total = links[0] * states[0][:, cols(h)].astype(F32)
    for j in range(1, REACH):
        fade = jnp.exp(jnp.full((1, DV), -rate * (SPAN * j), F32)) * links[j]
        total = total + fade * states[j][:, cols(h)].astype(F32)
    return total


def one_hot(target):
    return jnp.where(lax.broadcasted_iota(jnp.int32, (512, 512), 1) == target, 1.0, 0.0).astype(BF16)


def update_kernel(rate_ref, k_ref, v_ref, u_ref, sel_ref, order_ref):
    for h in range(HEADS):
        fade = jnp.exp(-rate_ref[h] * (SPAN - offsets()))
        k = k_ref[:, cols(h)].astype(F32) * fade
        u_ref[:, cols(h)] = tn(k, v_ref[:, cols(h)].astype(F32), PREC).astype(BF16)
    row = lax.broadcasted_iota(jnp.int32, (512, 1), 0)
    near = row // 128
    shift = jnp.where(near == 1, NEAR[1], jnp.where(near == 2, NEAR[2], jnp.where(near == 3, NEAR[3], NEAR[0])))
    z = (row // 32) % 4 * Z0 + (lax.axis_index("z0") + shift + Z0) % Z0
    sel_ref[...] = one_hot((row // 8) % 4 * 128 + (row // 4) % 2 * 64 + z * 4 + row % 4)
    order_ref[...] = one_hot((row // 64) % 2 * 256 + (row // 4) % 16 * 16 + row // 128 * 4 + row % 4)


def forward_kernel(rate_ref, spans_ref, q_ref, k_ref, v_ref, u1, u2, u3, normed_ref, rstd_ref, weights_ref, state_ref):
    links = joined(spans_ref, -1)
    for h in range(HEADS):
        rate = rate_ref[h]
        q, k, v = q_ref[:, cols(h)], k_ref[:, cols(h)], v_ref[:, cols(h)]
        weights = (nt(q, k) * SCALE * decay_mask(rate)).astype(BF16)
        weights_ref[:, cols(h)] = weights
        state = combined((u1, u2, u3), links, rate, h)
        state_ref[:, cols(h)] = state.astype(BF16)
        fade = SCALE * jnp.exp(-rate * offsets())
        out = nn(weights, v) + fade * nn(q.astype(F32), state, PREC)
        centred = out - jnp.mean(out, axis=1, keepdims=True)
        rstd = lax.rsqrt(jnp.mean(centred * centred, axis=1, keepdims=True) + EPS)
        normed_ref[:, cols(h)] = centred * rstd
        rstd_ref[:, h * 128 : (h + 1) * 128] = jnp.broadcast_to(rstd, (SPAN, 128))


def project_kernel(feat_ref, w0, w1, w2, w3, sel_ref, after_ref, out_ref, feat, sems):
    copies = []
    for y in range(Y):
        part = pl.ds(y * CORE, CORE)
        copies.append(pltpu.make_async_copy(feat_ref.at[part], feat.at[part], sems.at[y]))
        copies[y].start()
    rows = jnp.concatenate([w0[...], w1[...], w2[...], w3[...]], axis=0)
    weight = tn(rows, sel_ref[...]).astype(BF16)
    for y in range(Y):
        copies[y].wait()
        out = nn(feat[y * CORE], weight[:512, :]) + nn(feat[y * CORE + 1], weight[512:, :])
        high = out.astype(BF16)
        low = (out[:LOW] - high[:LOW].astype(F32)).astype(BF16)
        for x in range(X):
            out_ref[y * X + x, :SPAN] = high[:, x * 128 : (x + 1) * 128]
            out_ref[y * X + x, SPAN:] = low[:, x * 128 : (x + 1) * 128]


def norm_kernel(rate_ref, parts_ref, order_ref, normed_ref, rstd_ref, q_ref, g_ref, source_ref):
    sums = []
    for y in range(Y):
        total = parts_ref[y * X].astype(F32)
        for x in range(1, X):
            total = total + parts_ref[y * X + x].astype(F32)
        sums.append(jnp.concatenate([total[:LOW] + total[SPAN:], total[LOW:SPAN]], axis=0))
    whole = jnp.concatenate(sums, axis=1)
    high = whole.astype(BF16)
    low = (whole - high.astype(F32)).astype(BF16)
    norm_grad = nn(high, order_ref[...]) + nn(low, order_ref[...])
    for h in range(HEADS):
        grad = norm_grad[:, cols(h)]
        normed = normed_ref[:, cols(h)]
        rstd = rstd_ref[:, h * 128 : h * 128 + 1]
        inner = jnp.mean(normed * grad, axis=1, keepdims=True)
        g = rstd * (grad - jnp.mean(grad, axis=1, keepdims=True) - normed * inner)
        g_ref[:, cols(h)] = g.astype(BF16)
        fade = jnp.exp(-rate_ref[h] * offsets())
        source_ref[:, cols(h)] = tn(q_ref[:, cols(h)], (g * fade).astype(BF16)).astype(BF16)


def local_kernel(rate_ref, q_ref, k_ref, v_ref, g_ref, weights_ref, state_ref, qg_ref, kg_ref, vg_ref):
    for h in range(HEADS):
        rate = rate_ref[h]
        q, k, v, g = q_ref[:, cols(h)], k_ref[:, cols(h)], v_ref[:, cols(h)], g_ref[:, cols(h)]
        score = (nt(g, v) * decay_mask(rate)).astype(BF16)
        fade = jnp.exp(-rate * offsets())
        qg = nn(score, k) + fade * nt(g, state_ref[:, cols(h)])
        qg_ref[:, cols(h)] = (SCALE * qg).astype(BF16)
        kg_ref[:, cols(h)] = tn(score, q)
        vg_ref[:, cols(h)] = tn(weights_ref[:, cols(h)], g)


def final_kernel(rate_ref, spans_ref, s1, s2, s3, k_ref, v_ref, kg_ref, vg_ref, k_out, v_out):
    links = joined(spans_ref, 1)
    for h in range(HEADS):
        rate = rate_ref[h]
        later = combined((s1, s2, s3), links, rate, h).astype(BF16)
        fade = SCALE * jnp.exp(-rate * (SPAN - offsets()))
        k_out[:, cols(h)] = (SCALE * kg_ref[:, cols(h)] + fade * nt(v_ref[:, cols(h)], later)).astype(BF16)
        v_out[:, cols(h)] = (vg_ref[:, cols(h)] + fade * nn(k_ref[:, cols(h)], later)).astype(BF16)


def call(kernel, name, in_specs, outs, flops=0, room=32, **more):
    params = pltpu.CompilerParams(vmem_limit_bytes=room * 1024 * 1024)
    return pl.pallas_call(
        kernel,
        name=name,
        in_specs=in_specs,
        out_shape=outs,
        compiler_params=params,
        cost_estimate=pl.CostEstimate(flops=flops, bytes_accessed=2 << 20, transcendentals=0),
        **more,
    )


def sds(shape, dtype):
    return jax.ShapeDtypeStruct(shape, dtype)


def shift(x, axes, size, by):
    return lax.ppermute(x, axes, [(i, (i + by) % size) for i in range(size)])


def shards(queries, keys, values, out_grad, out_weight, decay_rate, doc_spans):
    block = (SPAN, HEADS * 256)
    split = jnp.broadcast_to(out_weight.reshape(8, X, 1024).transpose(1, 0, 2), (Z1, X, 8, 1024)).reshape(Z1 * X, 8, 1024)
    held = lax.all_to_all(split, ("z1", "x"), 0, 0).reshape(128, 1024)
    rows = [held] + [shift(held, DEPTH, Z, -s) for s in NEAR[1:]]
    features = lax.all_gather(out_grad, ("y", "core"), axis=0)

    update, sel, order = call(
        update_kernel,
        "update",
        [SMEM, VMEM, VMEM],
        [sds(block, BF16), sds((512, 512), BF16), sds((512, 512), BF16)],
        flops=1 << 28,
    )(decay_rate, keys, values)
    before = [shift(update, CTX, Z * Y, j) for j in range(1, REACH + 1)]
    normed, rstd, weights, state = call(
        forward_kernel,
        "forward",
        [SMEM, SMEM] + [VMEM] * 6,
        [sds(block, F32), sds((SPAN, 256), F32), sds(block, BF16), sds(block, BF16)],
        flops=1 << 29,
    )(decay_rate, doc_spans, queries, keys, values, *before)

    partial = call(
        project_kernel,
        "project",
        [HBM] + [VMEM] * 5 + [ANY],
        sds((Y * X, SENT, 128), BF16),
        flops=1 << 30,
        room=32,
        scratch_shapes=[pltpu.VMEM((Y * CORE, SPAN, 512), BF16), pltpu.SemaphoreType.DMA((Y,))],
    )(features, *rows, sel, state)
    parts = lax.all_to_all(partial, ("y", "x"), 0, 0)

    g, source = call(norm_kernel, "norm", [SMEM] + [VMEM] * 5, [sds(block, BF16)] * 2, flops=1 << 26)(
        decay_rate, parts, order, normed, rstd, queries
    )
    after = [shift(source, CTX, Z * Y, -j) for j in range(1, REACH + 1)]
    query_grad, kg, vg = call(
        local_kernel, "local", [SMEM] + [VMEM] * 6, [sds(block, BF16), sds(block, F32), sds(block, F32)], flops=1 << 28
    )(decay_rate, queries, keys, values, g, weights, state)
    key_grad, value_grad = call(final_kernel, "final", [SMEM, SMEM] + [VMEM] * 7, [sds(block, BF16)] * 2, flops=1 << 27)(
        decay_rate, doc_spans, *after, keys, values, kg, vg
    )
    return query_grad, key_grad, value_grad


def solution(mesh):
    fine = Mesh(mesh.devices.reshape(Z1, Z0, Y, X, CORE), ("z1", "z0", "y", "x", "core"))
    in_specs = (P(CTX, HEAD), P(CTX, HEAD), P(CTX, HEAD), P(CTX, HEAD), P(HEAD, CTX, None), P(HEAD), P())
    out_specs = (P(CTX, HEAD), P(CTX, HEAD), P(CTX, HEAD))
    return jax.shard_map(shards, mesh=fine, in_specs=in_specs, out_specs=out_specs, check_vma=False)
```

time: 892 us -> 129 us (0.14)
  waiting for transfers between devices: 562 us -> 15.5 us
  other arithmetic: 153 us -> 0 us
  blocking collectives: 124 us -> 22.6 us
  starting transfers between devices: 0.16 us -> 54.2 us
  matrix products: 17.2 us -> 0 us
  Pallas kernels: 0 us -> 11.9 us
    all_gather x4 -> x1, waiting for transfers between devices: 561 us -> 0.01 us  [shards(): features = lax.all_gather(out_grad, ('y', 'core'), axis=0)]
    select_n x128 -> x0, other arithmetic: 150 us -> none  [hop(): return jax.tree.map(lambda a, b: jnp.where(reached, a, b), new, before)]
    unnamed x1 -> x0, blocking collectives: 124 us -> none
    ppermute x0 -> x9, starting transfers between devices: none -> 35.9 us  [shift(): return lax.ppermute(x, axes, [(i, (i + by) % size) for i in range(size)])]
    all_to_all x0 -> x1, blocking collectives: none -> 22.6 us  [shards(): parts = lax.all_to_all(partial, ('y', 'x'), 0, 0)]
    all_to_all x0 -> x1, starting transfers between devices: none -> 18.2 us  [shards(): held = lax.all_to_all(split, ('z1', 'x'), 0, 0).reshape(128, 1024)]
    dot_general x13 -> x0, matrix products: 17.2 us -> none  [the longest x1 7.57 us: shards(): lax.dot_general(features_all, lax.all_gather(out_weight, 'ctx', axis=1, t...]
    pallas_call x0 -> x6, Pallas kernels: none -> 11.9 us  [the longest x1 2.67 us: shards(): call(project_kernel, 'project', [HBM] + [VMEM] * 5 + [ANY], sds((Y * X, S...]
  transfers between devices with their start and end apart: 4 -> 11, of which waited for: 3 -> 5; matrix products, arithmetic and copies ran while one was open for 9% -> 1% of each run, Pallas kernels for 0% -> 5%
where the time goes in v1:
time: 129 us; the launch traced here: 128 us
  starting transfers between devices  54.2 us (42%)
  blocking collectives  22.6 us (18%)
  waiting for transfers between devices  15.5 us (12%)
  between operations  14.3 us (11%)
  Pallas kernels  11.9 us (9%)
  local copies, waits for them, and re-layouts  9.62 us (7%)
    ppermute x9, starting transfers between devices, shift(): return lax.ppermute(x, axes, [(i, (i + by) % size) for i in range(size)])  35.9 us
    all_to_all x1, blocking collectives, shards(): parts = lax.all_to_all(partial, ('y', 'x'), 0, 0)  22.6 us
    all_to_all x1, starting transfers between devices, shards(): held = lax.all_to_all(split, ('z1', 'x'), 0, 0).reshape(128, 1024)  18.2 us
    ppermute x9, waiting for transfers between devices, shift(): return lax.ppermute(x, axes, [(i, (i + by) % size) for i in range(size)])  11.3 us
    unnamed x32, local copies, waits for them, and re-layouts  7.97 us
    all_to_all x1, waiting for transfers between devices, shards(): held = lax.all_to_all(split, ('z1', 'x'), 0, 0).reshape(128, 1024)  3.52 us
    pallas_call x1, Pallas kernels, shards(): call(project_kernel, 'project', [HBM] + [VMEM] * 5 + [ANY], sds((Y * X, S...  2.67 us
  transfers between devices with their start and end apart: 11, of which 5 were waited for; matrix products, arithmetic and copies ran while one was open for 1% of the time, Pallas kernels for 5%

profile of v1, /device:TPU:1, one launch (start us, length us, event | category | flops | bytes accessed | tf_op | source)
XLA Modules:
  0.0 128.1 jit_solution(18358143910556447144)
XLA Ops:
  9.6 18.2 %all-to-all-start = ((bf16[16,8,1024]{2,1,0:T(8,128)(2,1)}), bf16[16,8,1024]{2,1,0:T(8,128)(2,1)S(1)}, u32[]{:S(2)}, u32[]{:S(2)}) async-start(bf16[16,8,1024]{2,1,0:T(8,128)(2,1)} %bitcast.2), calls=%async_computation | async-start | bytes 524288 | tf_op jit(solution)/shard_map/all_to_all | solution.py:209
  27.9 1.8 %update.1 = (bf16[256,512]{1,0:T(8,128)(2,1)S(1)}, bf16[512,512]{1,0:T(8,128)(2,1)S(1)}, bf16[512,512]{1,0:T(8,128)(2,1)S(1)}) custom-call(f32[2]{0:T(128)S(1)} %copy-done.10, bf16[256,512]{1,0:T(8,128)(2,1)S(1)} %copy-done.2, bf16[256,512]{1,0:T(8,128)(2,1)S(1)} %copy-done.3), custom_call_target="tpu_custom_call" | custom-call | flops 268435456 | bytes 2097152 | tf_op jit(solution)/shard_map/update/pallas_call | solution.py:213
  29.7 4.6 %collective-permute-start.5 = (bf16[256,512]{1,0:T(8,128)(2,1)S(1)}, bf16[256,512]{1,0:T(8,128)(2,1)S(1)}, u32[]{:S(2)}, u32[]{:S(2)}) collective-permute-start(bf16[256,512]{1,0:T(8,128)(2,1)S(1)} %get-tuple-element.18), channel_id=1, source_target_pairs={{0,24},{8,32},{16,40},{24,48},{32,56},{40,64},{48,72},{56,80},{64,... | collective-permute-start | bytes 786440 | tf_op jit(solution)/shard_map/ppermute | solution.py:203
  34.3 2.7 %collective-permute-start.4 = (bf16[256,512]{1,0:T(8,128)(2,1)S(1)}, bf16[256,512]{1,0:T(8,128)(2,1)S(1)}, u32[]{:S(2)}, u32[]{:S(2)}) collective-permute-start(bf16[256,512]{1,0:T(8,128)(2,1)S(1)} %get-tuple-element.18), channel_id=1, source_target_pairs={{0,16},{8,24},{16,32},{24,40},{32,48},{40,56},{48,64},{56,72},{64,... | collective-permute-start | bytes 786440 | tf_op jit(solution)/shard_map/ppermute | solution.py:203
  37.1 2.6 %collective-permute-start.3 = (bf16[256,512]{1,0:T(8,128)(2,1)S(1)}, bf16[256,512]{1,0:T(8,128)(2,1)}, u32[]{:S(2)}, u32[]{:S(2)}) collective-permute-start(bf16[256,512]{1,0:T(8,128)(2,1)S(1)} %get-tuple-element.18), channel_id=1, source_target_pairs={{0,8},{8,16},{16,24},{24,32},{32,40},{40,48},{48,56},{56,64},{64,7... | collective-permute-start | bytes 786440 | tf_op jit(solution)/shard_map/ppermute | solution.py:203
  39.7 3.5 %all-to-all-done = bf16[16,8,1024]{2,1,0:T(8,128)(2,1)S(1)} async-done(((bf16[16,8,1024]{2,1,0:T(8,128)(2,1)}), bf16[16,8,1024]{2,1,0:T(8,128)(2,1)S(1)}, u32[]{:S(2)}, u32[]{:S(2)}) %all-to-all-start) | async-done | bytes 262176 | tf_op jit(solution)/shard_map/all_to_all | solution.py:209
  43.2 9.2 %collective-permute-start.2 = (bf16[128,1024]{1,0:T(8,128)(2,1)S(1)}, bf16[128,1024]{1,0:T(8,128)(2,1)S(1)}, u32[]{:S(2)}, u32[]{:S(2)}) collective-permute-start(bf16[128,1024]{1,0:T(8,128)(2,1)S(1)} %bitcast.5), channel_id=1, source_target_pairs={{0,448},{32,480},{64,0},{96,32},{128,64},{160,96},{192,128},{224,1... | collective-permute-start | bytes 786440 | tf_op jit(solution)/shard_map/ppermute | solution.py:203
  52.4 1.9 %collective-permute-start.1 = (bf16[128,1024]{1,0:T(8,128)(2,1)S(1)}, bf16[128,1024]{1,0:T(8,128)(2,1)S(1)}, u32[]{:S(2)}, u32[]{:S(2)}) collective-permute-start(bf16[128,1024]{1,0:T(8,128)(2,1)S(1)} %bitcast.6), channel_id=1, source_target_pairs={{0,32},{32,64},{64,96},{96,128},{128,160},{160,192},{192,224},{224... | collective-permute-start | bytes 786440 | tf_op jit(solution)/shard_map/ppermute | solution.py:203
  55.0 4.6 %collective-permute-start = (bf16[128,1024]{1,0:T(8,128)(2,1)S(1)}, bf16[128,1024]{1,0:T(8,128)(2,1)S(1)}, u32[]{:S(2)}, u32[]{:S(2)}) collective-permute-start(bf16[128,1024]{1,0:T(8,128)(2,1)S(1)} %bitcast.7), channel_id=1, source_target_pairs={{0,480},{32,0},{64,32},{96,64},{128,96},{160,128},{192,160},{224,1... | collective-permute-start | bytes 786440 | tf_op jit(solution)/shard_map/ppermute | solution.py:203
  60.3 3.1 %collective-permute-done.3.u1 = bf16[256,512]{1,0:T(8,128)(2,1)} collective-permute-done((bf16[256,512]{1,0:T(8,128)(2,1)S(1)}, bf16[256,512]{1,0:T(8,128)(2,1)}, u32[]{:S(2)}, u32[]{:S(2)}) %collective-permute-start.3) | collective-permute-done | bytes 262176 | tf_op jit(solution)/shard_map/ppermute | solution.py:203
  63.4 0.9 copy-done.13
  64.3 0.9 copy-done.15
  65.3 2.2 %forward.1 = (f32[256,512]{1,0:T(8,128)S(1)}, f32[256,256]{1,0:T(8,128)S(1)}, bf16[256,512]{1,0:T(8,128)(2,1)S(1)}, bf16[256,512]{1,0:T(8,128)(2,1)S(1)}) custom-call(f32[2]{0:T(128)S(1)} %copy-done.10, s32[21]{0:T(128)S(1)} %copy-done.11, bf16[256,512]{1,0:T(8,128)(2,1)S(1)} %copy-done.1, bf16[256,512]{1,0:T(8,128)(2,1)S(1)} %copy-done.2, ...), custom_call_target="tpu_custom_call" | custom-call | flops 536870912 | bytes 2097152 | tf_op jit(solution)/shard_map/forward/pallas_call | solution.py:221
  69.7 1.6 %copy-done = bf16[2048,512]{1,0:T(8,128)(2,1)S(1)} copy-done((bf16[2048,512]{1,0:T(8,128)(2,1)S(1)}, bf16[2048,512]{1,0:T(8,128)(2,1)}, u32[]{:S(2)}) %copy-start) | copy-done | bytes 2097176
  72.3 2.7 %project.1 = bf16[16,288,128]{2,1,0:T(8,128)(2,1)S(1)} custom-call(bf16[8,256,512]{2,1,0:T(8,128)(2,1)S(1)} %bitcast.4, bf16[128,1024]{1,0:T(8,128)(2,1)S(1)} %bitcast.8, bf16[128,1024]{1,0:T(8,128)(2,1)S(1)} %copy-done.5, bf16[128,1024]{1,0:T(8,128)(2,1)S(1)} %collective-permute-done.1.w2, bf16[128,1024]{1,0:T(8,128)(2,1)S(1)} %collective-permute-done.2.w3, ...), custom_call_target="tpu_custom_call" | custom-call | flops 1073741824 | bytes 2097152 | tf_op jit(solution)/shard_map/project/pallas_call | solution.py:229
  75.0 22.6 %all_to_all.10.parts_ref = bf16[16,288,128]{2,1,0:T(8,128)(2,1)S(1)} all-to-all(bf16[16,288,128]{2,1,0:T(8,128)(2,1)S(1)} %project.1), channel_id=1, replica_groups=mesh['z1'=4,'z0'=4,'y'=4,'x'=4,'core'=2] {'y','x'}, dimensions={0} | all-to-all | bytes 2359296 | tf_op jit(solution)/shard_map/all_to_all | solution.py:238
  97.6 1.5 %norm.1 = (bf16[256,512]{1,0:T(8,128)(2,1)S(1)}, bf16[256,512]{1,0:T(8,128)(2,1)S(1)}) custom-call(f32[2]{0:T(128)S(1)} %copy-done.10, bf16[16,288,128]{2,1,0:T(8,128)(2,1)S(1)} %all_to_all.10.parts_ref, bf16[512,512]{1,0:T(8,128)(2,1)S(1)} %get-tuple-element.20.order_ref, f32[256,512]{1,0:T(8,128)S(1)} %get-tuple-element.21.normed_ref, ...), custom_call_target="tpu_custom_call" | custom-call | flops 67108864 | bytes 2097152 | tf_op jit(solution)/shard_map/norm/pallas_call | solution.py:240
  99.1 3.0 %collective-permute-start.8 = (bf16[256,512]{1,0:T(8,128)(2,1)S(1)}, bf16[256,512]{1,0:T(8,128)(2,1)S(1)}, u32[]{:S(2)}, u32[]{:S(2)}) collective-permute-start(bf16[256,512]{1,0:T(8,128)(2,1)S(1)} %get-tuple-element.26), channel_id=1, source_target_pairs={{0,488},{8,496},{16,504},{24,0},{32,8},{40,16},{48,24},{56,32},{64... | collective-permute-start | bytes 786440 | tf_op jit(solution)/shard_map/ppermute | solution.py:203
  102.1 3.2 %collective-permute-start.7 = (bf16[256,512]{1,0:T(8,128)(2,1)S(1)}, bf16[256,512]{1,0:T(8,128)(2,1)S(1)}, u32[]{:S(2)}, u32[]{:S(2)}) collective-permute-start(bf16[256,512]{1,0:T(8,128)(2,1)S(1)} %get-tuple-element.26), channel_id=1, source_target_pairs={{0,496},{8,504},{16,0},{24,8},{32,16},{40,24},{48,32},{56,40},{64,... | collective-permute-start | bytes 786440 | tf_op jit(solution)/shard_map/ppermute | solution.py:203
  105.3 4.1 %collective-permute-start.6 = (bf16[256,512]{1,0:T(8,128)(2,1)S(1)}, bf16[256,512]{1,0:T(8,128)(2,1)S(1)}, u32[]{:S(2)}, u32[]{:S(2)}) collective-permute-start(bf16[256,512]{1,0:T(8,128)(2,1)S(1)} %get-tuple-element.26), channel_id=1, source_target_pairs={{0,504},{8,0},{16,8},{24,16},{32,24},{40,32},{48,40},{56,48},{64,5... | collective-permute-start | bytes 786440 | tf_op jit(solution)/shard_map/ppermute | solution.py:203
  109.4 1.9 %local.1 = (bf16[256,512]{1,0:T(8,128)(2,1)}, f32[256,512]{1,0:T(8,128)S(1)}, f32[256,512]{1,0:T(8,128)S(1)}) custom-call(f32[2]{0:T(128)S(1)} %copy-done.10, bf16[256,512]{1,0:T(8,128)(2,1)S(1)} %copy-done.1, bf16[256,512]{1,0:T(8,128)(2,1)S(1)} %copy-done.2, bf16[256,512]{1,0:T(8,128)(2,1)S(1)} %copy-done.3, bf16[256,512]{1,0:T(8,128)(2,1)S(1)} %get-tuple-element.23.g_ref, ...), custom_call_target="tpu_custom_call" | custom-call | flops 268435456 | bytes 2097152 | tf_op jit(solution)/shard_map/local/pallas_call | solution.py:244
  111.3 2.8 %collective-permute-done.7.s2 = bf16[256,512]{1,0:T(8,128)(2,1)S(1)} collective-permute-done((bf16[256,512]{1,0:T(8,128)(2,1)S(1)}, bf16[256,512]{1,0:T(8,128)(2,1)S(1)}, u32[]{:S(2)}, u32[]{:S(2)}) %collective-permute-start.7) | collective-permute-done | bytes 262176 | tf_op jit(solution)/shard_map/ppermute | solution.py:203
  114.2 5.2 %collective-permute-done.6.s1 = bf16[256,512]{1,0:T(8,128)(2,1)S(1)} collective-permute-done((bf16[256,512]{1,0:T(8,128)(2,1)S(1)}, bf16[256,512]{1,0:T(8,128)(2,1)S(1)}, u32[]{:S(2)}, u32[]{:S(2)}) %collective-permute-start.6) | collective-permute-done | bytes 262176 | tf_op jit(solution)/shard_map/ppermute | solution.py:203
  119.4 1.8 %final.1 = (bf16[256,512]{1,0:T(8,128)(2,1)}, bf16[256,512]{1,0:T(8,128)(2,1)}) custom-call(f32[2]{0:T(128)S(1)} %copy-done.10, s32[21]{0:T(128)S(1)} %copy-done.11, bf16[256,512]{1,0:T(8,128)(2,1)S(1)} %collective-permute-done.6.s1, bf16[256,512]{1,0:T(8,128)(2,1)S(1)} %collective-permute-done.7.s2, bf16[256,512]{1,0:T(8,128)(2,1)S(1)} %collective-permute-done.8.s3, ...), custom_call_target="tpu_custom_call" | custom-call | flops 134217728 | bytes 2097152 | tf_op jit(solution)/shard_map/final/pallas_call | solution.py:247
  (41 shorter events, 7.0 us)
Async XLA Ops:
  7.2 20.7 %copy-start.10 = (f32[2]{0:T(128)S(1)}, f32[2]{0:T(128)}, u32[]{:S(2)}) copy-start(f32[2]{0:T(128)} %rate_ref.9) | copy-start | bytes 28
  7.2 20.7 %copy-start.3 = (bf16[256,512]{1,0:T(8,128)(2,1)S(1)}, bf16[256,512]{1,0:T(8,128)(2,1)}, u32[]{:S(2)}) copy-start(bf16[256,512]{1,0:T(8,128)(2,1)} %v_ref.7) | copy-start | bytes 786436
  7.2 20.7 %copy-start.2 = (bf16[256,512]{1,0:T(8,128)(2,1)S(1)}, bf16[256,512]{1,0:T(8,128)(2,1)}, u32[]{:S(2)}) copy-start(bf16[256,512]{1,0:T(8,128)(2,1)} %k_ref.7) | copy-start | bytes 786436
  7.2 56.2 %copy-start.1 = (bf16[256,512]{1,0:T(8,128)(2,1)S(1)}, bf16[256,512]{1,0:T(8,128)(2,1)}, u32[]{:S(2)}) copy-start(bf16[256,512]{1,0:T(8,128)(2,1)} %q_ref.5) | copy-start | bytes 786436
  7.2 56.2 %copy-start.11 = (s32[21]{0:T(128)S(1)}, s32[21]{0:T(128)}, u32[]{:S(2)}) copy-start(s32[21]{0:T(128)} %spans_ref.3) | copy-start | bytes 256
  7.2 62.5 %all-gather.3.cloned.1.call-start = ((), (), s32[]{:S(2)}) async-start(), calls=%async_computation.2 | async-start | bytes 2359296 | tf_op jit(solution)/shard_map/all_gather | solution.py:211
  9.6 33.6 %all-to-all-start = ((bf16[16,8,1024]{2,1,0:T(8,128)(2,1)}), bf16[16,8,1024]{2,1,0:T(8,128)(2,1)S(1)}, u32[]{:S(2)}, u32[]{:S(2)}) async-start(bf16[16,8,1024]{2,1,0:T(8,128)(2,1)} %bitcast.2), calls=%async_computation | async-start | bytes 524288 | tf_op jit(solution)/shard_map/all_to_all | solution.py:209
  29.7 24.6 %collective-permute-start.5 = (bf16[256,512]{1,0:T(8,128)(2,1)S(1)}, bf16[256,512]{1,0:T(8,128)(2,1)S(1)}, u32[]{:S(2)}, u32[]{:S(2)}) collective-permute-start(bf16[256,512]{1,0:T(8,128)(2,1)S(1)} %get-tuple-element.18), channel_id=1, source_target_pairs={{0,24},{8,32},{16,40},{24,48},{32,56},{40,64},{48,72},{56,80},{64,... | collective-permute-start | bytes 786440 | tf_op jit(solution)/shard_map/ppermute | solution.py:203
  34.3 25.2 %collective-permute-start.4 = (bf16[256,512]{1,0:T(8,128)(2,1)S(1)}, bf16[256,512]{1,0:T(8,128)(2,1)S(1)}, u32[]{:S(2)}, u32[]{:S(2)}) collective-permute-start(bf16[256,512]{1,0:T(8,128)(2,1)S(1)} %get-tuple-element.18), channel_id=1, source_target_pairs={{0,16},{8,24},{16,32},{24,40},{32,48},{40,56},{48,64},{56,72},{64,... | collective-permute-start | bytes 786440 | tf_op jit(solution)/shard_map/ppermute | solution.py:203
  37.1 26.3 %collective-permute-start.3 = (bf16[256,512]{1,0:T(8,128)(2,1)S(1)}, bf16[256,512]{1,0:T(8,128)(2,1)}, u32[]{:S(2)}, u32[]{:S(2)}) collective-permute-start(bf16[256,512]{1,0:T(8,128)(2,1)S(1)} %get-tuple-element.18), channel_id=1, source_target_pairs={{0,8},{8,16},{16,24},{24,32},{32,40},{40,48},{48,56},{56,64},{64,7... | collective-permute-start | bytes 786440 | tf_op jit(solution)/shard_map/ppermute | solution.py:203
  43.2 25.7 %collective-permute-start.2 = (bf16[128,1024]{1,0:T(8,128)(2,1)S(1)}, bf16[128,1024]{1,0:T(8,128)(2,1)S(1)}, u32[]{:S(2)}, u32[]{:S(2)}) collective-permute-start(bf16[128,1024]{1,0:T(8,128)(2,1)S(1)} %bitcast.5), channel_id=1, source_target_pairs={{0,448},{32,480},{64,0},{96,32},{128,64},{160,96},{192,128},{224,1... | collective-permute-start | bytes 786440 | tf_op jit(solution)/shard_map/ppermute | solution.py:203
  52.4 16.5 %collective-permute-start.1 = (bf16[128,1024]{1,0:T(8,128)(2,1)S(1)}, bf16[128,1024]{1,0:T(8,128)(2,1)S(1)}, u32[]{:S(2)}, u32[]{:S(2)}) collective-permute-start(bf16[128,1024]{1,0:T(8,128)(2,1)S(1)} %bitcast.6), channel_id=1, source_target_pairs={{0,32},{32,64},{64,96},{96,128},{128,160},{160,192},{192,224},{224... | collective-permute-start | bytes 786440 | tf_op jit(solution)/shard_map/ppermute | solution.py:203
  54.3 0.7 copy-start.12
  55.0 14.0 %collective-permute-start = (bf16[128,1024]{1,0:T(8,128)(2,1)S(1)}, bf16[128,1024]{1,0:T(8,128)(2,1)S(1)}, u32[]{:S(2)}, u32[]{:S(2)}) collective-permute-start(bf16[128,1024]{1,0:T(8,128)(2,1)S(1)} %bitcast.7), channel_id=1, source_target_pairs={{0,480},{32,0},{64,32},{96,64},{128,96},{160,128},{192,160},{224,1... | collective-permute-start | bytes 786440 | tf_op jit(solution)/shard_map/ppermute | solution.py:203
  59.6 0.7 copy-start.14
  63.4 1.0 copy-start.13
  64.3 0.9 copy-start.15
  69.7 1.6 %copy-start = (bf16[2048,512]{1,0:T(8,128)(2,1)S(1)}, bf16[2048,512]{1,0:T(8,128)(2,1)}, u32[]{:S(2)}) copy-start(bf16[2048,512]{1,0:T(8,128)(2,1)} %all-gather.3.cloned.1.call-done) | copy-start | bytes 6291460
  71.3 0.9 copy-start.5
  74.9 22.6 %copy-start.7 = (f32[256,256]{1,0:T(8,128)S(1)}, f32[256,256]{1,0:T(8,128)}, u32[]{:S(2)}) copy-start(f32[256,256]{1,0:T(8,128)} %copy-done.6) | copy-start | bytes 786436
  97.6 11.8 %copy-start.9 = (bf16[256,512]{1,0:T(8,128)(2,1)S(1)}, bf16[256,512]{1,0:T(8,128)(2,1)}, u32[]{:S(2)}) copy-start(bf16[256,512]{1,0:T(8,128)(2,1)} %copy-done.8) | copy-start | bytes 786436
  99.1 12.3 %collective-permute-start.8 = (bf16[256,512]{1,0:T(8,128)(2,1)S(1)}, bf16[256,512]{1,0:T(8,128)(2,1)S(1)}, u32[]{:S(2)}, u32[]{:S(2)}) collective-permute-start(bf16[256,512]{1,0:T(8,128)(2,1)S(1)} %get-tuple-element.26), channel_id=1, source_target_pairs={{0,488},{8,496},{16,504},{24,0},{32,8},{40,16},{48,24},{56,32},{64... | collective-permute-start | bytes 786440 | tf_op jit(solution)/shard_map/ppermute | solution.py:203
  102.1 12.1 %collective-permute-start.7 = (bf16[256,512]{1,0:T(8,128)(2,1)S(1)}, bf16[256,512]{1,0:T(8,128)(2,1)S(1)}, u32[]{:S(2)}, u32[]{:S(2)}) collective-permute-start(bf16[256,512]{1,0:T(8,128)(2,1)S(1)} %get-tuple-element.26), channel_id=1, source_target_pairs={{0,496},{8,504},{16,0},{24,8},{32,16},{40,24},{48,32},{56,40},{64,... | collective-permute-start | bytes 786440 | tf_op jit(solution)/shard_map/ppermute | solution.py:203
  105.3 14.1 %collective-permute-start.6 = (bf16[256,512]{1,0:T(8,128)(2,1)S(1)}, bf16[256,512]{1,0:T(8,128)(2,1)S(1)}, u32[]{:S(2)}, u32[]{:S(2)}) collective-permute-start(bf16[256,512]{1,0:T(8,128)(2,1)S(1)} %get-tuple-element.26), channel_id=1, source_target_pairs={{0,504},{8,0},{16,8},{24,16},{32,24},{40,32},{48,40},{56,48},{64,5... | collective-permute-start | bytes 786440 | tf_op jit(solution)/shard_map/ppermute | solution.py:203
  (3 other events, 2.1 us)
Sparse Core Ops, SparseCore 0:
  10.2 47.0 all-gather.2

commit v2 on v1

v2 whole, which is shorter than its diff:
```python
import jax
import jax.numpy as jnp
from jax import lax
from jax.experimental import pallas as pl
from jax.experimental.pallas import tpu as pltpu
from jax.sharding import Mesh, PartitionSpec as P

DK = 256
DV = 256
SPAN = 256
HEADS = 2
REACH = 3
EPS = 1e-05
SCALE = DK**-0.5
F32 = jnp.float32
BF16 = jnp.bfloat16
PREC = lax.Precision.HIGHEST
NEAR = (0, 1, -1, 2)
LOW = 32
SENT = SPAN + LOW

Z1, Z0, Y, X, CORE = 4, 4, 4, 4, 2
Z = Z1 * Z0
DEPTH = ("z1", "z0")
CTX = ("z1", "z0", "y")
HEAD = ("x", "core")

SMEM = pl.BlockSpec(memory_space=pltpu.SMEM)
VMEM = pl.BlockSpec(memory_space=pltpu.VMEM)
ANY = pl.BlockSpec(memory_space=pl.ANY)
HBM = pl.BlockSpec(memory_space=pltpu.HBM)


def dot(a, b, dims, precision=None):
    return lax.dot_general(a, b, ((dims[:1], dims[1:]), ((), ())), precision=precision, preferred_element_type=F32)


def nn(a, b, precision=None):
    return dot(a, b, (1, 0), precision)


def nt(a, b, precision=None):
    return dot(a, b, (1, 1), precision)


def tn(a, b, precision=None):
    return dot(a, b, (0, 0), precision)


def cols(h):
    return slice(h * 256, (h + 1) * 256)


def offsets():
    return lax.broadcasted_iota(jnp.int32, (SPAN, 1), 0).astype(F32)


def decay_mask(rate):
    t = lax.broadcasted_iota(jnp.int32, (SPAN, SPAN), 0)
    s = lax.broadcasted_iota(jnp.int32, (SPAN, SPAN), 1)
    distance = jnp.maximum(t - s, 0).astype(F32)
    return jnp.where(t >= s, jnp.exp(-rate * distance), 0.0)


def joined(spans_ref, towards):
    place = (lax.axis_index("z1") * Z0 + lax.axis_index("z0")) * Y + lax.axis_index("y")
    edges = [place + 1 + j if towards > 0 else place - j for j in range(REACH)]
    cut = [jnp.int32(0)] * REACH
    first = jnp.int32(0)
    for i in range(spans_ref.shape[0] + 1):
        cut = [c + (first == e).astype(jnp.int32) for c, e in zip(cut, edges)]
        if i < spans_ref.shape[0]:
            first = first + spans_ref[i]
    out, total = [], jnp.int32(0)
    for c in cut:
        total = total + c
        out.append(jnp.where(total == 0, 1.0, 0.0).astype(F32))
    return out


def combined(states, links, rate, h):
    total = links[0] * states[0][:, cols(h)].astype(F32)
    for j in range(1, len(states)):
        fade = jnp.exp(jnp.full((1, DV), -rate * (SPAN * j), F32)) * links[j]
        total = total + fade * states[j][:, cols(h)].astype(F32)
    return total


def one_hot(target):
    return jnp.where(lax.broadcasted_iota(jnp.int32, (512, 512), 0) == target, 1.0, 0.0).astype(BF16)


def weight_order():
    row = lax.broadcasted_iota(jnp.int32, (1, 512), 1)
    near = row // 128
    shift = jnp.where(near == 1, NEAR[1], jnp.where(near == 2, NEAR[2], jnp.where(near == 3, NEAR[3], NEAR[0])))
    z = (row // 32) % 4 * Z0 + (lax.axis_index("z0") + shift + Z0) % Z0
    return one_hot((row // 8) % 4 * 128 + (row // 4) % 2 * 64 + z * 4 + row % 4)


def value_order():
    column = lax.broadcasted_iota(jnp.int32, (1, 512), 1)
    return one_hot((column // 4) % 4 * 128 + column // 256 * 64 + (column // 16) % 16 * 4 + column % 4)


def weights_of(q, k, rate):
    return (nt(q, k) * SCALE * decay_mask(rate)).astype(BF16)


def update_kernel(rate_ref, k_hbm, v_hbm, feat_ref, u_ref, own_ref, k_ref, v_ref, sems):
    pairs = ((k_hbm, k_ref), (v_hbm, v_ref), (feat_ref, own_ref))
    copies = [pltpu.make_async_copy(a, b, sems.at[i]) for i, (a, b) in enumerate(pairs)]
    for copy in copies:
        copy.start()
    for copy in copies:
        copy.wait()
    for h in range(HEADS):
        fade = jnp.exp(-rate_ref[h] * (SPAN - offsets()))
        k = k_ref[:, cols(h)].astype(F32) * fade
        u_ref[:, cols(h)] = tn(k, v_ref[:, cols(h)].astype(F32), PREC).astype(BF16)


def near_kernel(s0, s1, s2, s3, a0, out_ref):
    for i, span in enumerate((s0, s1, s2, s3)):
        out_ref[i * SPAN : (i + 1) * SPAN] = span[...]


def second_kernel(rate_ref, spans_ref, own, u1, after_ref, out_ref):
    link = joined(spans_ref, -1)[0]
    for h in range(HEADS):
        out_ref[:, cols(h)] = combined((own, u1), (1.0, link), rate_ref[h], h).astype(BF16)


def forward_kernel(rate_ref, spans_ref, q_ref, k_ref, v_ref, u1, u2, after_ref, normed_ref, state_ref):
    links = joined(spans_ref, -1)
    for h in range(HEADS):
        rate = rate_ref[h]
        q, k, v = q_ref[:, cols(h)], k_ref[:, cols(h)], v_ref[:, cols(h)]
        weights = weights_of(q, k, rate)
        state = combined((u1, u2), links, rate, h)
        state_ref[:, cols(h)] = state.astype(BF16)
        fade = SCALE * jnp.exp(-rate * offsets())
        out = nn(weights, v) + fade * nn(q.astype(F32), state, PREC)
        centred = out - jnp.mean(out, axis=1, keepdims=True)
        rstd = lax.rsqrt(jnp.mean(centred * centred, axis=1, keepdims=True) + EPS)
        normed_ref[:, cols(h)] = centred * rstd
        normed_ref[:, 512 + h * 64 : 576 + h * 64] = jnp.broadcast_to(rstd, (SPAN, 64))


def sort_kernel(w0, w1, w2, w3, out_ref):
    rows = jnp.concatenate([w0[...], w1[...], w2[...], w3[...]], axis=0)
    out_ref[...] = nn(weight_order(), rows).astype(BF16)


def project_kernel(f0, f1, weight_ref, after_ref, out_ref, feat, weight, sems):
    pairs = ((weight_ref, weight), (f0, feat.at[0]), (f1, feat.at[1]))
    copies = [pltpu.make_async_copy(a, b, sems.at[i]) for i, (a, b) in enumerate(pairs)]
    for copy in copies:
        copy.start()
    core = lax.axis_index("core")
    for copy in copies:
        copy.wait()
    for i in range(Y):
        out = jnp.zeros((SPAN, 512), F32)
        for half in range(CORE):
            column = pl.multiple_of(lax.rem(core + half, CORE) * 512, 512)
            out += nt(feat[half, i * SPAN : (i + 1) * SPAN], weight[:, pl.ds(column, 512)])
        high = out.astype(BF16)
        low = (out[:LOW] - high[:LOW].astype(F32)).astype(BF16)
        place = lax.rem(lax.axis_index("y") + i, Y) * X
        for x in range(X):
            out_ref[place + x, :SPAN] = high[:, x * 128 : (x + 1) * 128]
            out_ref[place + x, SPAN:] = low[:, x * 128 : (x + 1) * 128]


def norm_kernel(rate_ref, parts_ref, normed_ref, q_ref, g_ref, source_ref):
    order = value_order()
    sums = []
    for y in range(Y):
        total = parts_ref[y * X].astype(F32)
        for x in range(1, X):
            total = total + parts_ref[y * X + x].astype(F32)
        sums.append(jnp.concatenate([total[:LOW] + total[SPAN:], total[LOW:SPAN]], axis=0))
    whole = jnp.concatenate(sums, axis=1)
    high = whole.astype(BF16)
    low = (whole - high.astype(F32)).astype(BF16)
    norm_grad = nn(high, order) + nn(low, order)
    for h in range(HEADS):
        grad = norm_grad[:, cols(h)]
        normed = normed_ref[:, cols(h)]
        rstd = normed_ref[:, 512 + h * 64 : 513 + h * 64]
        inner = jnp.mean(normed * grad, axis=1, keepdims=True)
        g = rstd * (grad - jnp.mean(grad, axis=1, keepdims=True) - normed * inner)
        g_ref[:, cols(h)] = g.astype(BF16)
        fade = jnp.exp(-rate_ref[h] * offsets())
        source_ref[:, cols(h)] = tn(q_ref[:, cols(h)], (g * fade).astype(BF16)).astype(BF16)


def local_kernel(rate_ref, q_ref, k_ref, v_ref, g_ref, state_ref, qg_ref, kg_ref, vg_ref):
    for h in range(HEADS):
        rate = rate_ref[h]
        q, k, v, g = q_ref[:, cols(h)], k_ref[:, cols(h)], v_ref[:, cols(h)], g_ref[:, cols(h)]
        score = (nt(g, v) * decay_mask(rate)).astype(BF16)
        fade = jnp.exp(-rate * offsets())
        qg = nn(score, k) + fade * nt(g, state_ref[:, cols(h)])
        qg_ref[:, cols(h)] = (SCALE * qg).astype(BF16)
        kg_ref[:, cols(h)] = tn(score, q)
        vg_ref[:, cols(h)] = tn(weights_of(q, k, rate), g)


def final_kernel(rate_ref, spans_ref, s1, s2, s3, k_ref, v_ref, kg_ref, vg_ref, k_out, v_out):
    links = joined(spans_ref, 1)
    for h in range(HEADS):
        rate = rate_ref[h]
        later = combined((s1, s2, s3), links, rate, h).astype(BF16)
        fade = SCALE * jnp.exp(-rate * (SPAN - offsets()))
        k_out[:, cols(h)] = (SCALE * kg_ref[:, cols(h)] + fade * nt(v_ref[:, cols(h)], later)).astype(BF16)
        v_out[:, cols(h)] = (vg_ref[:, cols(h)] + fade * nn(k_ref[:, cols(h)], later)).astype(BF16)


def call(kernel, name, in_specs, outs, flops=0, room=32, **more):
    params = pltpu.CompilerParams(vmem_limit_bytes=room * 1024 * 1024)
    return pl.pallas_call(
        kernel,
        name=name,
        in_specs=in_specs,
        out_shape=outs,
        compiler_params=params,
        cost_estimate=pl.CostEstimate(flops=flops, bytes_accessed=2 << 20, transcendentals=0),
        **more,
    )


def sds(shape, dtype):
    return jax.ShapeDtypeStruct(shape, dtype)


def shift(x, axes, size, by):
    return lax.ppermute(x, axes, [(i, (i + by) % size) for i in range(size)])


def shards(queries, keys, values, out_grad, out_weight, decay_rate, doc_spans):
    block = (SPAN, HEADS * 256)
    split = jnp.broadcast_to(out_weight.reshape(8, X, 1024).transpose(1, 0, 2), (Z1, X, 8, 1024))
    held = lax.all_to_all(split.reshape(Z1 * X, 8, 1024), ("z1", "x"), 0, 0).reshape(128, 1024)
    update, own = call(
        update_kernel,
        "update",
        [SMEM] + [HBM] * 3,
        [sds(block, BF16)] * 2,
        flops=1 << 28,
        scratch_shapes=[pltpu.VMEM(block, BF16), pltpu.VMEM(block, BF16), pltpu.SemaphoreType.DMA((3,))],
    )(decay_rate, *[pltpu.with_memory_space_constraint(x, pltpu.HBM) for x in (keys, values, out_grad)])
    spans = [own] + [shift(own, "y", Y, -j) for j in range(1, Y)]
    u1 = shift(update, CTX, Z * Y, 1)
    second = call(second_kernel, "second", [SMEM, SMEM, VMEM, VMEM, ANY], sds(block, BF16), flops=1 << 20)(
        decay_rate, doc_spans, update, u1, held
    )
    u2 = shift(second, CTX, Z * Y, 2)
    rows = [held] + [shift(held, DEPTH, Z, -s) for s in NEAR[1:]]
    near = call(near_kernel, "near", [VMEM] * 4 + [ANY] * 1, sds((Y * SPAN, 512), BF16))(*spans, held)
    weight = call(sort_kernel, "sort", [VMEM] * 4, sds((512, 1024), BF16), flops=1 << 34)(*rows)
    features = [near, shift(near, "core", CORE, 1)]

    partial = call(
        project_kernel,
        "project",
        [ANY] * 4,
        sds((Y * X, SENT, 128), BF16),
        flops=1 << 30,
        room=32,
        scratch_shapes=[
            pltpu.VMEM((CORE, Y * SPAN, 512), BF16),
            pltpu.VMEM((512, 1024), BF16),
            pltpu.SemaphoreType.DMA((3,)),
        ],
    )(*features, weight, u2)
    normed, state = call(
        forward_kernel,
        "forward",
        [SMEM, SMEM] + [VMEM] * 5 + [ANY],
        [sds((SPAN, 640), F32), sds(block, BF16)],
        flops=1 << 29,
    )(decay_rate, doc_spans, queries, keys, values, u1, u2, partial)
    parts = lax.all_to_all(partial, ("y", "x"), 0, 0)

    g, source = call(norm_kernel, "norm", [SMEM] + [VMEM] * 3, [sds(block, BF16)] * 2, flops=1 << 26)(
        decay_rate, parts, normed, queries
    )
    after = [shift(source, CTX, Z * Y, -j) for j in range(1, REACH + 1)]
    query_grad, kg, vg = call(
        local_kernel, "local", [SMEM] + [VMEM] * 5, [sds(block, BF16), sds(block, F32), sds(block, F32)], flops=1 << 28
    )(decay_rate, queries, keys, values, g, state)
    key_grad, value_grad = call(final_kernel, "final", [SMEM, SMEM] + [VMEM] * 7, [sds(block, BF16)] * 2, flops=1 << 27)(
        decay_rate, doc_spans, *after, keys, values, kg, vg
    )
    return query_grad, key_grad, value_grad


def solution(mesh):
    fine = Mesh(mesh.devices.reshape(Z1, Z0, Y, X, CORE), ("z1", "z0", "y", "x", "core"))
    in_specs = (P(CTX, HEAD), P(CTX, HEAD), P(CTX, HEAD), P(CTX, HEAD), P(HEAD, CTX, None), P(HEAD), P())
    out_specs = (P(CTX, HEAD), P(CTX, HEAD), P(CTX, HEAD))
    return jax.shard_map(shards, mesh=fine, in_specs=in_specs, out_specs=out_specs, check_vma=False)
```

time: 129 us -> 115 us (0.89)
  blocking collectives: 22.6 us -> 0 us
  starting transfers between devices: 54.2 us -> 73 us
  between operations: 14.3 us -> 0.94 us
  waiting for transfers between devices: 15.5 us -> 23.9 us
  local copies, waits for them, and re-layouts: 9.62 us -> 2.34 us
  Pallas kernels: 11.9 us -> 13.6 us
    all_to_all x1 -> x0, blocking collectives: 22.6 us -> none  [shards(): parts = lax.all_to_all(partial, ('y', 'x'), 0, 0)]
    ppermute x9 -> x12, starting transfers between devices: 35.9 us -> 50.7 us  [shift(): return lax.ppermute(x, axes, [(i, (i + by) % size) for i in range(size)])]
    all_to_all x1 -> x2, waiting for transfers between devices: 3.52 us -> 13.6 us  [the longest x1 13.6 us: shards(): parts = lax.all_to_all(partial, ('y', 'x'), 0, 0)]
    unnamed x32 -> x12, local copies, waits for them, and re-layouts: 7.97 us -> 0.68 us
    all_to_all x1 -> x2, starting transfers between devices: 18.2 us -> 22.2 us  [the longest x1 18.2 us: shards(): lax.all_to_all(split.reshape(Z1 * X, 8, 1024), ('z1', 'x'), 0, 0)]
    pallas_call x5 -> x8, Pallas kernels: 10.1 us -> 11.8 us  [the longest x1 2.59 us: shards(): call(project_kernel, 'project', [ANY] * 4, sds((Y * X, SENT, 128), BF16),...]
    ppermute x9 -> x12, waiting for transfers between devices: 11.3 us -> 10.3 us  [shift(): return lax.ppermute(x, axes, [(i, (i + by) % size) for i in range(size)])]
  transfers between devices with their start and end apart: 11 -> 14, of which waited for: 5 -> 5; matrix products, arithmetic and copies ran while one was open for 1% -> 0% of each run, Pallas kernels for 5% -> 7%
where the time goes in v2:
time: 115 us; the launch traced here: 114 us
  starting transfers between devices  73 us (63%)
  waiting for transfers between devices  23.9 us (21%)
  Pallas kernels  13.6 us (12%)
  local copies, waits for them, and re-layouts  2.34 us (2%)
    ppermute x12, starting transfers between devices, shift(): return lax.ppermute(x, axes, [(i, (i + by) % size) for i in range(size)])  50.7 us
    all_to_all x1, starting transfers between devices, shards(): lax.all_to_all(split.reshape(Z1 * X, 8, 1024), ('z1', 'x'), 0, 0)  18.2 us
    all_to_all x1, waiting for transfers between devices, shards(): parts = lax.all_to_all(partial, ('y', 'x'), 0, 0)  13.6 us
    ppermute x12, waiting for transfers between devices, shift(): return lax.ppermute(x, axes, [(i, (i + by) % size) for i in range(size)])  10.3 us
    all_to_all x1, starting transfers between devices, shards(): parts = lax.all_to_all(partial, ('y', 'x'), 0, 0)  4.04 us
    pallas_call x1, Pallas kernels, shards(): call(project_kernel, 'project', [ANY] * 4, sds((Y * X, SENT, 128), BF16),...  2.59 us
    pallas_call x1, Pallas kernels, shards(): call(update_kernel, 'update', [SMEM] + [HBM] * 3, [sds(block, BF16)] * 2,...  2.42 us
  transfers between devices with their start and end apart: 14, of which 5 were waited for; matrix products, arithmetic and copies ran while one was open for 0% of the time, Pallas kernels for 7%

profile of v2, /device:TPU:1, one launch (start us, length us, event | category | flops | bytes accessed | tf_op | source)
XLA Modules:
  0.0 113.7 jit_solution(10484129942124850946)
XLA Ops:
  2.3 18.2 %all-to-all-start = ((bf16[16,8,1024]{2,1,0:T(8,128)(2,1)}), bf16[16,8,1024]{2,1,0:T(8,128)(2,1)S(1)}, u32[]{:S(2)}, u32[]{:S(2)}) async-start(bf16[16,8,1024]{2,1,0:T(8,128)(2,1)} %bitcast.1), calls=%async_computation | async-start | bytes 524288 | tf_op jit(solution)/shard_map/all_to_all | solution.py:245
  21.2 2.4 %update.1 = (bf16[256,512]{1,0:T(8,128)(2,1)S(1)}, bf16[256,512]{1,0:T(8,128)(2,1)S(1)}) custom-call(f32[2]{0:T(128)S(1)} %copy-done.3, bf16[256,512]{1,0:T(8,128)(2,1)} %k_ref.5, bf16[256,512]{1,0:T(8,128)(2,1)} %v_ref.5, bf16[256,512]{1,0:T(8,128)(2,1)} %feat_ref.1), custom_call_target="tpu_custom_call" | custom-call | flops 268435456 | bytes 2097152 | tf_op jit(solution)/shard_map/update/pallas_call | solution.py:246
  23.6 3.2 %collective-permute-start.7 = (bf16[256,512]{1,0:T(8,128)(2,1)S(1)}, bf16[256,512]{1,0:T(8,128)(2,1)S(1)}, u32[]{:S(2)}, u32[]{:S(2)}) collective-permute-start(bf16[256,512]{1,0:T(8,128)(2,1)S(1)} %get-tuple-element.15.own), channel_id=1, source_target_pairs={{0,8},{8,16},{16,24},{24,32},{32,40},{40,48},{48,56},{56,64},{64,7... | collective-permute-start | bytes 786440 | tf_op jit(solution)/shard_map/ppermute | solution.py:239
  26.8 3.2 %collective-permute-start.2 = (bf16[256,512]{1,0:T(8,128)(2,1)S(1)}, bf16[256,512]{1,0:T(8,128)(2,1)S(1)}, u32[]{:S(2)}, u32[]{:S(2)}) collective-permute-start(bf16[256,512]{1,0:T(8,128)(2,1)S(1)} %get-tuple-element.14.s0), channel_id=1, source_target_pairs={{0,8},{8,16},{16,24},{24,0},{1,9},{9,17},{17,25},{25,1},{2,10},{10... | collective-permute-start | bytes 786440 | tf_op jit(solution)/shard_map/ppermute | solution.py:239
  30.0 3.6 %collective-permute-start.1 = (bf16[256,512]{1,0:T(8,128)(2,1)S(1)}, bf16[256,512]{1,0:T(8,128)(2,1)S(1)}, u32[]{:S(2)}, u32[]{:S(2)}) collective-permute-start(bf16[256,512]{1,0:T(8,128)(2,1)S(1)} %get-tuple-element.14.s0), channel_id=1, source_target_pairs={{0,16},{8,24},{16,0},{24,8},{1,17},{9,25},{17,1},{25,9},{2,18},{10... | collective-permute-start | bytes 786440 | tf_op jit(solution)/shard_map/ppermute | solution.py:239
  33.7 3.6 %collective-permute-start = (bf16[256,512]{1,0:T(8,128)(2,1)S(1)}, bf16[256,512]{1,0:T(8,128)(2,1)S(1)}, u32[]{:S(2)}, u32[]{:S(2)}) collective-permute-start(bf16[256,512]{1,0:T(8,128)(2,1)S(1)} %get-tuple-element.14.s0), channel_id=1, source_target_pairs={{0,24},{8,0},{16,8},{24,16},{1,25},{9,1},{17,9},{25,17},{2,26},{10... | collective-permute-start | bytes 786440 | tf_op jit(solution)/shard_map/ppermute | solution.py:239
  37.3 7.8 %collective-permute-start.6 = (bf16[128,1024]{1,0:T(8,128)(2,1)S(1)}, bf16[128,1024]{1,0:T(8,128)(2,1)S(1)}, u32[]{:S(2)}, u32[]{:S(2)}) collective-permute-start(bf16[128,1024]{1,0:T(8,128)(2,1)S(1)} %bitcast.3), channel_id=1, source_target_pairs={{0,448},{32,480},{64,0},{96,32},{128,64},{160,96},{192,128},{224,1... | collective-permute-start | bytes 786440 | tf_op jit(solution)/shard_map/ppermute | solution.py:239
  45.4 1.9 %collective-permute-start.5 = (bf16[128,1024]{1,0:T(8,128)(2,1)S(1)}, bf16[128,1024]{1,0:T(8,128)(2,1)S(1)}, u32[]{:S(2)}, u32[]{:S(2)}) collective-permute-start(bf16[128,1024]{1,0:T(8,128)(2,1)S(1)} %bitcast.4), channel_id=1, source_target_pairs={{0,32},{32,64},{64,96},{96,128},{128,160},{160,192},{192,224},{224... | collective-permute-start | bytes 786440 | tf_op jit(solution)/shard_map/ppermute | solution.py:239
  47.3 6.6 %collective-permute-start.4 = (bf16[128,1024]{1,0:T(8,128)(2,1)S(1)}, bf16[128,1024]{1,0:T(8,128)(2,1)S(1)}, u32[]{:S(2)}, u32[]{:S(2)}) collective-permute-start(bf16[128,1024]{1,0:T(8,128)(2,1)S(1)} %bitcast.5), channel_id=1, source_target_pairs={{0,480},{32,0},{64,32},{96,64},{128,96},{160,128},{192,160},{224,1... | collective-permute-start | bytes 786440 | tf_op jit(solution)/shard_map/ppermute | solution.py:239
  54.6 2.5 %collective-permute-start.8 = (bf16[256,512]{1,0:T(8,128)(2,1)S(1)}, bf16[256,512]{1,0:T(8,128)(2,1)S(1)}, u32[]{:S(2)}, u32[]{:S(2)}) collective-permute-start(bf16[256,512]{1,0:T(8,128)(2,1)S(1)} %second.1), channel_id=1, source_target_pairs={{0,16},{8,24},{16,32},{24,40},{32,48},{40,56},{48,64},{56,72},{64,... | collective-permute-start | bytes 786440 | tf_op jit(solution)/shard_map/ppermute | solution.py:239
  57.2 4.9 %collective-permute-start.3 = (bf16[1024,512]{1,0:T(8,128)(2,1)S(1)}, bf16[1024,512]{1,0:T(8,128)(2,1)S(1)}, u32[]{:S(2)}, u32[]{:S(2)}) collective-permute-start(bf16[1024,512]{1,0:T(8,128)(2,1)S(1)} %near.1.f0), channel_id=1, source_target_pairs={{0,1},{1,0},{2,3},{3,2},{4,5},{5,4},{6,7},{7,6},{8,9},{9,8},{10,11... | collective-permute-start | bytes 3145736 | tf_op jit(solution)/shard_map/ppermute | solution.py:239
  62.9 2.9 %collective-permute-done.8.after_ref.u2 = bf16[256,512]{1,0:T(8,128)(2,1)S(1)} collective-permute-done((bf16[256,512]{1,0:T(8,128)(2,1)S(1)}, bf16[256,512]{1,0:T(8,128)(2,1)S(1)}, u32[]{:S(2)}, u32[]{:S(2)}) %collective-permute-start.8) | collective-permute-done | bytes 262176 | tf_op jit(solution)/shard_map/ppermute | solution.py:239
  65.8 2.6 %project.1.after_ref = bf16[16,288,128]{2,1,0:T(8,128)(2,1)} custom-call(bf16[1024,512]{1,0:T(8,128)(2,1)S(1)} %near.1.f0, bf16[1024,512]{1,0:T(8,128)(2,1)S(1)} %collective-permute-done.3.f1, bf16[512,1024]{1,0:T(8,128)(2,1)S(1)} %sort.1.weight_ref, bf16[256,512]{1,0:T(8,128)(2,1)S(1)} %collective-permute-done.8.after_ref.u2), custom_call_target="tpu_custom_call" | custom-call | flops 1073741824 | bytes 2097152 | tf_op jit(solution)/shard_map/project/pallas_call | solution.py:265
  68.4 4.0 %all-to-all-start.1 = ((bf16[16,288,128]{2,1,0:T(8,128)(2,1)}), bf16[16,288,128]{2,1,0:T(8,128)(2,1)S(1)}, u32[]{:S(2)}, u32[]{:S(2)}) async-start(bf16[16,288,128]{2,1,0:T(8,128)(2,1)} %project.1.after_ref), calls=%async_computation.1 | async-start | bytes 2359296 | tf_op jit(solution)/shard_map/all_to_all | solution.py:285
  72.5 1.7 %forward.1 = (f32[256,640]{1,0:T(8,128)S(1)}, bf16[256,512]{1,0:T(8,128)(2,1)S(1)}) custom-call(f32[2]{0:T(128)S(1)} %copy-done.4, s32[21]{0:T(128)S(1)} %copy-done.5, bf16[256,512]{1,0:T(8,128)(2,1)S(1)} %copy-done, bf16[256,512]{1,0:T(8,128)(2,1)S(1)} %copy-done.1, bf16[256,512]{1,0:T(8,128)(2,1)S(1)} %copy-done.2, ...), custom_call_target="tpu_custom_call" | custom-call | flops 536870912 | bytes 2097152 | tf_op jit(solution)/shard_map/forward/pallas_call | solution.py:278
  74.2 13.6 %all-to-all-done.1.parts_ref = bf16[16,288,128]{2,1,0:T(8,128)(2,1)S(1)} async-done(((bf16[16,288,128]{2,1,0:T(8,128)(2,1)}), bf16[16,288,128]{2,1,0:T(8,128)(2,1)S(1)}, u32[]{:S(2)}, u32[]{:S(2)}) %all-to-all-start.1) | async-done | bytes 1179680 | tf_op jit(solution)/shard_map/all_to_all | solution.py:285
  87.8 1.6 %norm.1 = (bf16[256,512]{1,0:T(8,128)(2,1)S(1)}, bf16[256,512]{1,0:T(8,128)(2,1)S(1)}) custom-call(f32[2]{0:T(128)S(1)} %copy-done.4, bf16[16,288,128]{2,1,0:T(8,128)(2,1)S(1)} %all-to-all-done.1.parts_ref, f32[256,640]{1,0:T(8,128)S(1)} %get-tuple-element.16.normed_ref, bf16[256,512]{1,0:T(8,128)(2,1)S(1)} %copy-done), custom_call_target="tpu_custom_call" | custom-call | flops 67108864 | bytes 2097152 | tf_op jit(solution)/shard_map/norm/pallas_call | solution.py:287
  89.4 6.3 %collective-permute-start.11 = (bf16[256,512]{1,0:T(8,128)(2,1)S(1)}, bf16[256,512]{1,0:T(8,128)(2,1)S(1)}, u32[]{:S(2)}, u32[]{:S(2)}) collective-permute-start(bf16[256,512]{1,0:T(8,128)(2,1)S(1)} %get-tuple-element.20), channel_id=1, source_target_pairs={{0,488},{8,496},{16,504},{24,0},{32,8},{40,16},{48,24},{56,32},{64... | collective-permute-start | bytes 786440 | tf_op jit(solution)/shard_map/ppermute | solution.py:239
  95.7 3.1 %collective-permute-start.10 = (bf16[256,512]{1,0:T(8,128)(2,1)S(1)}, bf16[256,512]{1,0:T(8,128)(2,1)S(1)}, u32[]{:S(2)}, u32[]{:S(2)}) collective-permute-start(bf16[256,512]{1,0:T(8,128)(2,1)S(1)} %get-tuple-element.20), channel_id=1, source_target_pairs={{0,496},{8,504},{16,0},{24,8},{32,16},{40,24},{48,32},{56,40},{64,... | collective-permute-start | bytes 786440 | tf_op jit(solution)/shard_map/ppermute | solution.py:239
  98.8 4.0 %collective-permute-start.9 = (bf16[256,512]{1,0:T(8,128)(2,1)S(1)}, bf16[256,512]{1,0:T(8,128)(2,1)S(1)}, u32[]{:S(2)}, u32[]{:S(2)}) collective-permute-start(bf16[256,512]{1,0:T(8,128)(2,1)S(1)} %get-tuple-element.20), channel_id=1, source_target_pairs={{0,504},{8,0},{16,8},{24,16},{32,24},{40,32},{48,40},{56,48},{64,5... | collective-permute-start | bytes 786440 | tf_op jit(solution)/shard_map/ppermute | solution.py:239
  102.9 2.0 %local.1 = (bf16[256,512]{1,0:T(8,128)(2,1)}, f32[256,512]{1,0:T(8,128)S(1)}, f32[256,512]{1,0:T(8,128)S(1)}) custom-call(f32[2]{0:T(128)S(1)} %copy-done.4, bf16[256,512]{1,0:T(8,128)(2,1)S(1)} %copy-done, bf16[256,512]{1,0:T(8,128)(2,1)S(1)} %copy-done.1, bf16[256,512]{1,0:T(8,128)(2,1)S(1)} %copy-done.2, bf16[256,512]{1,0:T(8,128)(2,1)S(1)} %get-tuple-element.17.g_ref, ...), custom_call_target="tpu_custom_call" | custom-call | flops 268435456 | bytes 2097152 | tf_op jit(solution)/shard_map/local/pallas_call | solution.py:291
  104.9 2.8 %collective-permute-done.10.s2 = bf16[256,512]{1,0:T(8,128)(2,1)S(1)} collective-permute-done((bf16[256,512]{1,0:T(8,128)(2,1)S(1)}, bf16[256,512]{1,0:T(8,128)(2,1)S(1)}, u32[]{:S(2)}, u32[]{:S(2)}) %collective-permute-start.10) | collective-permute-done | bytes 262176 | tf_op jit(solution)/shard_map/ppermute | solution.py:239
  107.7 4.2 %collective-permute-done.9.s1 = bf16[256,512]{1,0:T(8,128)(2,1)S(1)} collective-permute-done((bf16[256,512]{1,0:T(8,128)(2,1)S(1)}, bf16[256,512]{1,0:T(8,128)(2,1)S(1)}, u32[]{:S(2)}, u32[]{:S(2)}) %collective-permute-start.9) | collective-permute-done | bytes 262176 | tf_op jit(solution)/shard_map/ppermute | solution.py:239
  111.9 1.8 %final.1 = (bf16[256,512]{1,0:T(8,128)(2,1)}, bf16[256,512]{1,0:T(8,128)(2,1)}) custom-call(f32[2]{0:T(128)S(1)} %copy-done.4, s32[21]{0:T(128)S(1)} %copy-done.5, bf16[256,512]{1,0:T(8,128)(2,1)S(1)} %collective-permute-done.9.s1, bf16[256,512]{1,0:T(8,128)(2,1)S(1)} %collective-permute-done.10.s2, bf16[256,512]{1,0:T(8,128)(2,1)S(1)} %collective-permute-done.11.s3, ...), custom_call_target="tpu_custom_call" | custom-call | flops 134217728 | bytes 2097152 | tf_op jit(solution)/shard_map/final/pallas_call | solution.py:294
  (28 shorter events, 4.1 us)
Async XLA Ops:
  0.6 53.3 %copy-start.4 = (f32[2]{0:T(128)S(1)}, f32[2]{0:T(128)}, u32[]{:S(2)}) copy-start(f32[2]{0:T(128)} %rate_ref.11) | copy-start | bytes 28
  0.6 53.3 %copy-start.5 = (s32[21]{0:T(128)S(1)}, s32[21]{0:T(128)}, u32[]{:S(2)}) copy-start(s32[21]{0:T(128)} %spans_ref.5) | copy-start | bytes 256
  2.3 35.0 %all-to-all-start = ((bf16[16,8,1024]{2,1,0:T(8,128)(2,1)}), bf16[16,8,1024]{2,1,0:T(8,128)(2,1)S(1)}, u32[]{:S(2)}, u32[]{:S(2)}) async-start(bf16[16,8,1024]{2,1,0:T(8,128)(2,1)} %bitcast.1), calls=%async_computation | async-start | bytes 524288 | tf_op jit(solution)/shard_map/all_to_all | solution.py:245
  20.5 0.7 copy-start.3
  23.6 21.8 %collective-permute-start.7 = (bf16[256,512]{1,0:T(8,128)(2,1)S(1)}, bf16[256,512]{1,0:T(8,128)(2,1)S(1)}, u32[]{:S(2)}, u32[]{:S(2)}) collective-permute-start(bf16[256,512]{1,0:T(8,128)(2,1)S(1)} %get-tuple-element.15.own), channel_id=1, source_target_pairs={{0,8},{8,16},{16,24},{24,32},{32,40},{40,48},{48,56},{56,64},{64,7... | collective-permute-start | bytes 786440 | tf_op jit(solution)/shard_map/ppermute | solution.py:239
  26.8 20.5 %collective-permute-start.2 = (bf16[256,512]{1,0:T(8,128)(2,1)S(1)}, bf16[256,512]{1,0:T(8,128)(2,1)S(1)}, u32[]{:S(2)}, u32[]{:S(2)}) collective-permute-start(bf16[256,512]{1,0:T(8,128)(2,1)S(1)} %get-tuple-element.14.s0), channel_id=1, source_target_pairs={{0,8},{8,16},{16,24},{24,0},{1,9},{9,17},{17,25},{25,1},{2,10},{10... | collective-permute-start | bytes 786440 | tf_op jit(solution)/shard_map/ppermute | solution.py:239
  30.0 24.6 %collective-permute-start.1 = (bf16[256,512]{1,0:T(8,128)(2,1)S(1)}, bf16[256,512]{1,0:T(8,128)(2,1)S(1)}, u32[]{:S(2)}, u32[]{:S(2)}) collective-permute-start(bf16[256,512]{1,0:T(8,128)(2,1)S(1)} %get-tuple-element.14.s0), channel_id=1, source_target_pairs={{0,16},{8,24},{16,0},{24,8},{1,17},{9,25},{17,1},{25,9},{2,18},{10... | collective-permute-start | bytes 786440 | tf_op jit(solution)/shard_map/ppermute | solution.py:239
  33.7 23.5 %collective-permute-start = (bf16[256,512]{1,0:T(8,128)(2,1)S(1)}, bf16[256,512]{1,0:T(8,128)(2,1)S(1)}, u32[]{:S(2)}, u32[]{:S(2)}) collective-permute-start(bf16[256,512]{1,0:T(8,128)(2,1)S(1)} %get-tuple-element.14.s0), channel_id=1, source_target_pairs={{0,24},{8,0},{16,8},{24,16},{1,25},{9,1},{17,9},{25,17},{2,26},{10... | collective-permute-start | bytes 786440 | tf_op jit(solution)/shard_map/ppermute | solution.py:239
  37.3 24.9 %collective-permute-start.6 = (bf16[128,1024]{1,0:T(8,128)(2,1)S(1)}, bf16[128,1024]{1,0:T(8,128)(2,1)S(1)}, u32[]{:S(2)}, u32[]{:S(2)}) collective-permute-start(bf16[128,1024]{1,0:T(8,128)(2,1)S(1)} %bitcast.3), channel_id=1, source_target_pairs={{0,448},{32,480},{64,0},{96,32},{128,64},{160,96},{192,128},{224,1... | collective-permute-start | bytes 786440 | tf_op jit(solution)/shard_map/ppermute | solution.py:239
  45.4 16.7 %collective-permute-start.5 = (bf16[128,1024]{1,0:T(8,128)(2,1)S(1)}, bf16[128,1024]{1,0:T(8,128)(2,1)S(1)}, u32[]{:S(2)}, u32[]{:S(2)}) collective-permute-start(bf16[128,1024]{1,0:T(8,128)(2,1)S(1)} %bitcast.4), channel_id=1, source_target_pairs={{0,32},{32,64},{64,96},{96,128},{128,160},{160,192},{192,224},{224... | collective-permute-start | bytes 786440 | tf_op jit(solution)/shard_map/ppermute | solution.py:239
  47.3 14.8 %collective-permute-start.4 = (bf16[128,1024]{1,0:T(8,128)(2,1)S(1)}, bf16[128,1024]{1,0:T(8,128)(2,1)S(1)}, u32[]{:S(2)}, u32[]{:S(2)}) collective-permute-start(bf16[128,1024]{1,0:T(8,128)(2,1)S(1)} %bitcast.5), channel_id=1, source_target_pairs={{0,480},{32,0},{64,32},{96,64},{128,96},{160,128},{192,160},{224,1... | collective-permute-start | bytes 786440 | tf_op jit(solution)/shard_map/ppermute | solution.py:239
  54.6 11.2 %collective-permute-start.8 = (bf16[256,512]{1,0:T(8,128)(2,1)S(1)}, bf16[256,512]{1,0:T(8,128)(2,1)S(1)}, u32[]{:S(2)}, u32[]{:S(2)}) collective-permute-start(bf16[256,512]{1,0:T(8,128)(2,1)S(1)} %second.1), channel_id=1, source_target_pairs={{0,16},{8,24},{16,32},{24,40},{32,48},{40,56},{48,64},{56,72},{64,... | collective-permute-start | bytes 786440 | tf_op jit(solution)/shard_map/ppermute | solution.py:239
  57.2 8.6 %collective-permute-start.3 = (bf16[1024,512]{1,0:T(8,128)(2,1)S(1)}, bf16[1024,512]{1,0:T(8,128)(2,1)S(1)}, u32[]{:S(2)}, u32[]{:S(2)}) collective-permute-start(bf16[1024,512]{1,0:T(8,128)(2,1)S(1)} %near.1.f0), channel_id=1, source_target_pairs={{0,1},{1,0},{2,3},{3,2},{4,5},{5,4},{6,7},{7,6},{8,9},{9,8},{10,11... | collective-permute-start | bytes 3145736 | tf_op jit(solution)/shard_map/ppermute | solution.py:239
  68.4 4.1 %copy-start = (bf16[256,512]{1,0:T(8,128)(2,1)S(1)}, bf16[256,512]{1,0:T(8,128)(2,1)}, u32[]{:S(2)}) copy-start(bf16[256,512]{1,0:T(8,128)(2,1)} %q_ref.5) | copy-start | bytes 786436
  68.4 4.1 %copy-start.1 = (bf16[256,512]{1,0:T(8,128)(2,1)S(1)}, bf16[256,512]{1,0:T(8,128)(2,1)}, u32[]{:S(2)}) copy-start(bf16[256,512]{1,0:T(8,128)(2,1)} %k_ref.5) | copy-start | bytes 786436
  68.4 4.1 %copy-start.2 = (bf16[256,512]{1,0:T(8,128)(2,1)S(1)}, bf16[256,512]{1,0:T(8,128)(2,1)}, u32[]{:S(2)}) copy-start(bf16[256,512]{1,0:T(8,128)(2,1)} %v_ref.5) | copy-start | bytes 786436
  68.4 19.3 %all-to-all-start.1 = ((bf16[16,288,128]{2,1,0:T(8,128)(2,1)}), bf16[16,288,128]{2,1,0:T(8,128)(2,1)S(1)}, u32[]{:S(2)}, u32[]{:S(2)}) async-start(bf16[16,288,128]{2,1,0:T(8,128)(2,1)} %project.1.after_ref), calls=%async_computation.1 | async-start | bytes 2359296 | tf_op jit(solution)/shard_map/all_to_all | solution.py:285
  89.4 15.5 %collective-permute-start.11 = (bf16[256,512]{1,0:T(8,128)(2,1)S(1)}, bf16[256,512]{1,0:T(8,128)(2,1)S(1)}, u32[]{:S(2)}, u32[]{:S(2)}) collective-permute-start(bf16[256,512]{1,0:T(8,128)(2,1)S(1)} %get-tuple-element.20), channel_id=1, source_target_pairs={{0,488},{8,496},{16,504},{24,0},{32,8},{40,16},{48,24},{56,32},{64... | collective-permute-start | bytes 786440 | tf_op jit(solution)/shard_map/ppermute | solution.py:239
  95.7 12.0 %collective-permute-start.10 = (bf16[256,512]{1,0:T(8,128)(2,1)S(1)}, bf16[256,512]{1,0:T(8,128)(2,1)S(1)}, u32[]{:S(2)}, u32[]{:S(2)}) collective-permute-start(bf16[256,512]{1,0:T(8,128)(2,1)S(1)} %get-tuple-element.20), channel_id=1, source_target_pairs={{0,496},{8,504},{16,0},{24,8},{32,16},{40,24},{48,32},{56,40},{64,... | collective-permute-start | bytes 786440 | tf_op jit(solution)/shard_map/ppermute | solution.py:239
  98.8 13.0 %collective-permute-start.9 = (bf16[256,512]{1,0:T(8,128)(2,1)S(1)}, bf16[256,512]{1,0:T(8,128)(2,1)S(1)}, u32[]{:S(2)}, u32[]{:S(2)}) collective-permute-start(bf16[256,512]{1,0:T(8,128)(2,1)S(1)} %get-tuple-element.20), channel_id=1, source_target_pairs={{0,504},{8,0},{16,8},{24,16},{32,24},{40,32},{48,40},{56,48},{64,5... | collective-permute-start | bytes 786440 | tf_op jit(solution)/shard_map/ppermute | solution.py:239

commit v3 on v2

--- a/solution.py
+++ b/solution.py
@@ -78,14 +78,6 @@
     return out
 
 
-def combined(states, links, rate, h):
-    total = links[0] * states[0][:, cols(h)].astype(F32)
-    for j in range(1, len(states)):
-        fade = jnp.exp(jnp.full((1, DV), -rate * (SPAN * j), F32)) * links[j]
-        total = total + fade * states[j][:, cols(h)].astype(F32)
-    return total
-
-
 def one_hot(target):
     return jnp.where(lax.broadcasted_iota(jnp.int32, (512, 512), 0) == target, 1.0, 0.0).astype(BF16)
 
@@ -105,6 +97,11 @@
 
 def weights_of(q, k, rate):
     return (nt(q, k) * SCALE * decay_mask(rate)).astype(BF16)
+
+
+def scales(aux, h):
+    later = [aux[SPAN + 2 * j + h : SPAN + 2 * j + h + 1, :1] for j in range(REACH)]
+    return aux[:SPAN, h : h + 1], aux[:SPAN, 2 + h : 3 + h], later
 
 
 def update_kernel(rate_ref, k_hbm, v_hbm, feat_ref, u_ref, own_ref, k_ref, v_ref, sems):
@@ -116,31 +113,52 @@
         copy.wait()
     for h in range(HEADS):
         fade = jnp.exp(-rate_ref[h] * (SPAN - offsets()))
-        k = k_ref[:, cols(h)].astype(F32) * fade
-        u_ref[:, cols(h)] = tn(k, v_ref[:, cols(h)].astype(F32), PREC).astype(BF16)
-
-
-def near_kernel(s0, s1, s2, s3, a0, out_ref):
+        k, v = k_ref[:, cols(h)].astype(F32) * fade, v_ref[:, cols(h)]
+        high = k.astype(BF16)
+        low = (k - high.astype(F32)).astype(BF16)
+        u_ref[:, cols(h)] = (tn(high, v) + tn(low, v)).astype(BF16)
+
+
+def split_kernel(w_hbm, out_ref, w_ref, sem):
+    copy = pltpu.make_async_copy(w_hbm, w_ref, sem)
+    copy.start()
+    copy.wait()
+    w = w_ref[...].astype(F32)
+    rows = jnp.concatenate([w[h] for h in range(HEADS)], axis=0).astype(BF16)
+    for z in range(Z1):
+        for x in range(X):
+            out_ref[z * X + x] = rows[:, x * 1024 : (x + 1) * 1024]
+
+
+def near_kernel(s0, s1, s3, s2, after_ref, out_ref):
     for i, span in enumerate((s0, s1, s2, s3)):
         out_ref[i * SPAN : (i + 1) * SPAN] = span[...]
 
 
-def second_kernel(rate_ref, spans_ref, own, u1, after_ref, out_ref):
-    link = joined(spans_ref, -1)[0]
-    for h in range(HEADS):
-        out_ref[:, cols(h)] = combined((own, u1), (1.0, link), rate_ref[h], h).astype(BF16)
-
-
-def forward_kernel(rate_ref, spans_ref, q_ref, k_ref, v_ref, u1, u2, after_ref, normed_ref, state_ref):
-    links = joined(spans_ref, -1)
-    for h in range(HEADS):
-        rate = rate_ref[h]
+def second_kernel(rate_ref, spans_ref, own, u1, after_ref, out_ref, aux_ref):
+    before, after = joined(spans_ref, -1), joined(spans_ref, 1)
+    lane = lax.broadcasted_iota(jnp.int32, (SPAN, 128), 1)
+    rate = jnp.where(lane % 2 == 0, rate_ref[0], rate_ref[1])
+    offset = lax.broadcasted_iota(jnp.int32, (SPAN, 128), 0)
+    aux_ref[:SPAN] = jnp.exp(-rate * jnp.where(lane < 2, offset, SPAN - offset).astype(F32))
+    row = lax.broadcasted_iota(jnp.int32, (8, 128), 0)
+    lane = lax.broadcasted_iota(jnp.int32, (8, 128), 1)
+    rate = jnp.where(row % 2 == 0, rate_ref[0], rate_ref[1])
+    links = [jnp.where(row // 2 == 0, c[0], jnp.where(row // 2 == 1, c[1], c[2])) for c in (before, after)]
+    aux_ref[SPAN:] = jnp.exp(-rate * (SPAN * (row // 2)).astype(F32)) * jnp.where(lane == 0, links[1], links[0])
+    for h in range(HEADS):
+        fade = jnp.exp(jnp.full((1, DV), -rate_ref[h] * SPAN, F32)) * before[0]
+        out_ref[:, cols(h)] = (own[:, cols(h)].astype(F32) + fade * u1[:, cols(h)].astype(F32)).astype(BF16)
+
+
+def forward_kernel(rate_ref, aux, q_ref, k_ref, v_ref, u1, u2, after_ref, normed_ref, state_ref):
+    for h in range(HEADS):
         q, k, v = q_ref[:, cols(h)], k_ref[:, cols(h)], v_ref[:, cols(h)]
-        weights = weights_of(q, k, rate)
-        state = combined((u1, u2), links, rate, h)
+        weights = weights_of(q, k, rate_ref[h])
+        state = aux[SPAN + h : SPAN + h + 1, 1:2] * u1[:, cols(h)].astype(F32)
+        state += aux[SPAN + 2 + h : SPAN + 3 + h, 1:2] * u2[:, cols(h)].astype(F32)
         state_ref[:, cols(h)] = state.astype(BF16)
-        fade = SCALE * jnp.exp(-rate * offsets())
-        out = nn(weights, v) + fade * nn(q.astype(F32), state, PREC)
+        out = nn(weights, v) + SCALE * scales(aux, h)[0] * nn(q.astype(F32), state, PREC)
         centred = out - jnp.mean(out, axis=1, keepdims=True)
         rstd = lax.rsqrt(jnp.mean(centred * centred, axis=1, keepdims=True) + EPS)
         normed_ref[:, cols(h)] = centred * rstd
@@ -152,28 +170,31 @@
     out_ref[...] = nn(weight_order(), rows).astype(BF16)
 
 
-def project_kernel(f0, f1, weight_ref, after_ref, out_ref, feat, weight, sems):
-    pairs = ((weight_ref, weight), (f0, feat.at[0]), (f1, feat.at[1]))
-    copies = [pltpu.make_async_copy(a, b, sems.at[i]) for i, (a, b) in enumerate(pairs)]
-    for copy in copies:
-        copy.start()
+def project_kernel(f0, f1, weight_ref, out_ref, sums, sems):
     core = lax.axis_index("core")
+    copies = []
+    for i in range(Y):
+        out = jnp.zeros((SPAN, 512), F32)
+        for half, feat in enumerate((f0, f1)):
+            column = pl.multiple_of(lax.rem(core + half, CORE) * 512, 512)
+            out += nt(feat[i * SPAN : (i + 1) * SPAN], weight_ref[:, pl.ds(column, 512)])
+        high = out.astype(BF16)
+        low = (out[:LOW] - high[:LOW].astype(F32)).astype(BF16)
+        for x in range(X):
+            sums[i * X + x, :SPAN] = high[:, x * 128 : (x + 1) * 128]
+            sums[i * X + x, SPAN:] = low[:, x * 128 : (x + 1) * 128]
+        place = lax.rem(lax.axis_index("y") + i, Y) * X
+        copies.append(pltpu.make_async_copy(sums.at[pl.ds(i * X, X)], out_ref.at[pl.ds(place, X)], sems.at[i]))
+        copies[i].start()
     for copy in copies:
         copy.wait()
-    for i in range(Y):
-        out = jnp.zeros((SPAN, 512), F32)
-        for half in range(CORE):
-            column = pl.multiple_of(lax.rem(core + half, CORE) * 512, 512)
-            out += nt(feat[half, i * SPAN : (i + 1) * SPAN], weight[:, pl.ds(column, 512)])
-        high = out.astype(BF16)
-        low = (out[:LOW] - high[:LOW].astype(F32)).astype(BF16)
-        place = lax.rem(lax.axis_index("y") + i, Y) * X
-        for x in range(X):
-            out_ref[place + x, :SPAN] = high[:, x * 128 : (x + 1) * 128]
-            out_ref[place + x, SPAN:] = low[:, x * 128 : (x + 1) * 128]
-
-
-def norm_kernel(rate_ref, parts_ref, normed_ref, q_ref, g_ref, source_ref):
+
+
+def gate_kernel(parts_ref, after_ref, out_ref):
+    pass
+
+
+def norm_kernel(aux, parts_ref, normed_ref, q_ref, g_ref, source_ref):
     order = value_order()
     sums = []
     for y in range(Y):
@@ -192,8 +213,7 @@
         inner = jnp.mean(normed * grad, axis=1, keepdims=True)
         g = rstd * (grad - jnp.mean(grad, axis=1, keepdims=True) - normed * inner)
         g_ref[:, cols(h)] = g.astype(BF16)
-        fade = jnp.exp(-rate_ref[h] * offsets())
-        source_ref[:, cols(h)] = tn(q_ref[:, cols(h)], (g * fade).astype(BF16)).astype(BF16)
+        source_ref[:, cols(h)] = tn(q_ref[:, cols(h)], (g * scales(aux, h)[0]).astype(BF16)).astype(BF16)
 
 
 def local_kernel(rate_ref, q_ref, k_ref, v_ref, g_ref, state_ref, qg_ref, kg_ref, vg_ref):
@@ -208,14 +228,19 @@
         vg_ref[:, cols(h)] = tn(weights_of(q, k, rate), g)
 
 
-def final_kernel(rate_ref, spans_ref, s1, s2, s3, k_ref, v_ref, kg_ref, vg_ref, k_out, v_out):
-    links = joined(spans_ref, 1)
-    for h in range(HEADS):
-        rate = rate_ref[h]
-        later = combined((s1, s2, s3), links, rate, h).astype(BF16)
-        fade = SCALE * jnp.exp(-rate * (SPAN - offsets()))
-        k_out[:, cols(h)] = (SCALE * kg_ref[:, cols(h)] + fade * nt(v_ref[:, cols(h)], later)).astype(BF16)
-        v_out[:, cols(h)] = (vg_ref[:, cols(h)] + fade * nn(k_ref[:, cols(h)], later)).astype(BF16)
+def final_kernel(aux, s1, s2, s3, k_ref, v_ref, kg_ref, vg_ref, k_out, v_out, k_done, v_done, sems):
+    copies = []
+    for h in range(HEADS):
+        fade, weights = scales(aux, h)[1:]
+        later = sum(w * state[:, cols(h)].astype(F32) for w, state in zip(weights, (s1, s2, s3))).astype(BF16)
+        fade = SCALE * fade
+        k_done[h] = (SCALE * kg_ref[:, cols(h)] + fade * nt(v_ref[:, cols(h)], later)).astype(BF16)
+        v_done[h] = (vg_ref[:, cols(h)] + fade * nn(k_ref[:, cols(h)], later)).astype(BF16)
+        for i, (done, out) in enumerate(((k_done, k_out), (v_done, v_out))):
+            copies.append(pltpu.make_async_copy(done.at[h], out.at[:, pl.ds(h * 256, 256)], sems.at[2 * h + i]))
+            copies[-1].start()
+    for copy in copies:
+        copy.wait()
 
 
 def call(kernel, name, in_specs, outs, flops=0, room=32, **more):
@@ -241,8 +266,14 @@
 
 def shards(queries, keys, values, out_grad, out_weight, decay_rate, doc_spans):
     block = (SPAN, HEADS * 256)
-    split = jnp.broadcast_to(out_weight.reshape(8, X, 1024).transpose(1, 0, 2), (Z1, X, 8, 1024))
-    held = lax.all_to_all(split.reshape(Z1 * X, 8, 1024), ("z1", "x"), 0, 0).reshape(128, 1024)
+    split = call(
+        split_kernel,
+        "split",
+        [HBM],
+        sds((Z1 * X, 8, 1024), BF16),
+        scratch_shapes=[pltpu.VMEM(out_weight.shape, BF16), pltpu.SemaphoreType.DMA],
+    )(pltpu.with_memory_space_constraint(out_weight, pltpu.HBM))
+    held = lax.all_to_all(split, ("z1", "x"), 0, 0).reshape(128, 1024)
     update, own = call(
         update_kernel,
         "update",
@@ -253,47 +284,59 @@
     )(decay_rate, *[pltpu.with_memory_space_constraint(x, pltpu.HBM) for x in (keys, values, out_grad)])
     spans = [own] + [shift(own, "y", Y, -j) for j in range(1, Y)]
     u1 = shift(update, CTX, Z * Y, 1)
-    second = call(second_kernel, "second", [SMEM, SMEM, VMEM, VMEM, ANY], sds(block, BF16), flops=1 << 20)(
-        decay_rate, doc_spans, update, u1, held
-    )
+    second, aux = call(
+        second_kernel,
+        "second",
+        [SMEM, SMEM, VMEM, VMEM, ANY],
+        [sds(block, BF16), sds((SPAN + 8, 128), F32)],
+        flops=1 << 20,
+    )(decay_rate, doc_spans, update, u1, held)
     u2 = shift(second, CTX, Z * Y, 2)
     rows = [held] + [shift(held, DEPTH, Z, -s) for s in NEAR[1:]]
-    near = call(near_kernel, "near", [VMEM] * 4 + [ANY] * 1, sds((Y * SPAN, 512), BF16))(*spans, held)
     weight = call(sort_kernel, "sort", [VMEM] * 4, sds((512, 1024), BF16), flops=1 << 34)(*rows)
+    near = call(near_kernel, "near", [VMEM] * 4 + [ANY], sds((Y * SPAN, 512), BF16))(
+        spans[0], spans[1], spans[3], spans[2], second
+    )
     features = [near, shift(near, "core", CORE, 1)]
 
     partial = call(
         project_kernel,
         "project",
-        [ANY] * 4,
+        [VMEM] * 3,
         sds((Y * X, SENT, 128), BF16),
         flops=1 << 30,
         room=32,
-        scratch_shapes=[
-            pltpu.VMEM((CORE, Y * SPAN, 512), BF16),
-            pltpu.VMEM((512, 1024), BF16),
-            pltpu.SemaphoreType.DMA((3,)),
-        ],
-    )(*features, weight, u2)
+        out_specs=HBM,
+        scratch_shapes=[pltpu.VMEM((Y * X, SENT, 128), BF16), pltpu.SemaphoreType.DMA((Y,))],
+    )(*features, weight)
+    partial = call(
+        gate_kernel, "gate", [ANY, ANY], sds((Y * X, SENT, 128), BF16), out_specs=ANY, input_output_aliases={0: 0}
+    )(partial, u2)
     normed, state = call(
         forward_kernel,
         "forward",
-        [SMEM, SMEM] + [VMEM] * 5 + [ANY],
+        [SMEM] + [VMEM] * 6 + [ANY],
         [sds((SPAN, 640), F32), sds(block, BF16)],
         flops=1 << 29,
-    )(decay_rate, doc_spans, queries, keys, values, u1, u2, partial)
+    )(decay_rate, aux, queries, keys, values, u1, u2, partial)
     parts = lax.all_to_all(partial, ("y", "x"), 0, 0)
 
-    g, source = call(norm_kernel, "norm", [SMEM] + [VMEM] * 3, [sds(block, BF16)] * 2, flops=1 << 26)(
-        decay_rate, parts, normed, queries
+    g, source = call(norm_kernel, "norm", [VMEM] * 4, [sds(block, BF16)] * 2, flops=1 << 26)(
+        aux, parts, normed, queries
     )
     after = [shift(source, CTX, Z * Y, -j) for j in range(1, REACH + 1)]
     query_grad, kg, vg = call(
         local_kernel, "local", [SMEM] + [VMEM] * 5, [sds(block, BF16), sds(block, F32), sds(block, F32)], flops=1 << 28
     )(decay_rate, queries, keys, values, g, state)
-    key_grad, value_grad = call(final_kernel, "final", [SMEM, SMEM] + [VMEM] * 7, [sds(block, BF16)] * 2, flops=1 << 27)(
-        decay_rate, doc_spans, *after, keys, values, kg, vg
-    )
+    key_grad, value_grad = call(
+        final_kernel,
+        "final",
+        [VMEM] * 8,
+        [sds(block, BF16)] * 2,
+        flops=1 << 27,
+        out_specs=[HBM, HBM],
+        scratch_shapes=[pltpu.VMEM((HEADS, SPAN, 256), BF16)] * 2 + [pltpu.SemaphoreType.DMA((4,))],
+    )(aux, *after, keys, values, kg, vg)
     return query_grad, key_grad, value_grad
 
 

time: 115 us -> 112 us (0.974)
  starting transfers between devices: 73 us -> 70.2 us
  local copies, waits for them, and re-layouts: 2.34 us -> 0.68 us
  waiting for transfers between devices: 23.9 us -> 25.5 us
    ppermute x12, starting transfers between devices: 50.7 us -> 48.2 us  [shift(): return lax.ppermute(x, axes, [(i, (i + by) % size) for i in range(size)])]
    pallas_call x6 -> x8, Pallas kernels: 8.43 us -> 8.51 us  [the longest x1 2.05 us: shards(): call(project_kernel, 'project', [VMEM] * 3, sds((Y * X, SENT, 128), BF16)...]
  transfers between devices with their start and end apart: 14 -> 14, of which waited for: 5 -> 5; matrix products, arithmetic and copies ran while one was open for 0% -> 0% of each run, Pallas kernels for 7% -> 9%
where the time goes in v3:
time: 112 us; the launch traced here: 111 us
  starting transfers between devices  70.2 us (63%)
  waiting for transfers between devices  25.5 us (23%)
  Pallas kernels  13.3 us (12%)
    ppermute x12, starting transfers between devices, shift(): return lax.ppermute(x, axes, [(i, (i + by) % size) for i in range(size)])  48.2 us
    all_to_all x1, starting transfers between devices, shards(): held = lax.all_to_all(split, ('z1', 'x'), 0, 0).reshape(128, 1024)  18.2 us
    all_to_all x1, waiting for transfers between devices, shards(): parts = lax.all_to_all(partial, ('y', 'x'), 0, 0)  14.7 us
    ppermute x12, waiting for transfers between devices, shift(): return lax.ppermute(x, axes, [(i, (i + by) % size) for i in range(size)])  10.8 us
    all_to_all x1, starting transfers between devices, shards(): parts = lax.all_to_all(partial, ('y', 'x'), 0, 0)  3.84 us
  transfers between devices with their start and end apart: 14, of which 5 were waited for; matrix products, arithmetic and copies ran while one was open for 0% of the time, Pallas kernels for 9%

profile of v3, /device:TPU:1, one launch (start us, length us, event | category | flops | bytes accessed | tf_op | source)
XLA Modules:
  0.0 110.7 jit_solution(7318488637578180785)
XLA Ops:
  0.7 1.6 %split.1 = bf16[16,8,1024]{2,1,0:T(8,128)(2,1)} custom-call(bf16[2,4,4096]{2,1,0:T(4,128)(2,1)} %w_hbm.1), custom_call_target="tpu_custom_call" | custom-call | bytes 2097152 | tf_op jit(solution)/shard_map/split/pallas_call | solution.py:269
  2.2 18.2 %all-to-all-start = ((bf16[16,8,1024]{2,1,0:T(8,128)(2,1)}), bf16[16,8,1024]{2,1,0:T(8,128)(2,1)S(1)}, u32[]{:S(2)}, u32[]{:S(2)}) async-start(bf16[16,8,1024]{2,1,0:T(8,128)(2,1)} %split.1), calls=%async_computation | async-start | bytes 524288 | tf_op jit(solution)/shard_map/all_to_all | solution.py:276
  21.1 2.1 %update.1 = (bf16[256,512]{1,0:T(8,128)(2,1)S(1)}, bf16[256,512]{1,0:T(8,128)(2,1)S(1)}) custom-call(f32[2]{0:T(128)S(1)} %copy-done.3, bf16[256,512]{1,0:T(8,128)(2,1)} %k_ref.5, bf16[256,512]{1,0:T(8,128)(2,1)} %v_ref.5, bf16[256,512]{1,0:T(8,128)(2,1)} %feat_ref.1), custom_call_target="tpu_custom_call" | custom-call | flops 268435456 | bytes 2097152 | tf_op jit(solution)/shard_map/update/pallas_call | solution.py:277
  23.2 3.2 %collective-permute-start = (bf16[256,512]{1,0:T(8,128)(2,1)S(1)}, bf16[256,512]{1,0:T(8,128)(2,1)S(1)}, u32[]{:S(2)}, u32[]{:S(2)}) collective-permute-start(bf16[256,512]{1,0:T(8,128)(2,1)S(1)} %get-tuple-element.16.own), channel_id=1, source_target_pairs={{0,8},{8,16},{16,24},{24,32},{32,40},{40,48},{48,56},{56,64},{64,7... | collective-permute-start | bytes 786440 | tf_op jit(solution)/shard_map/ppermute | solution.py:264
  26.4 4.5 %collective-permute-start.3 = (bf16[256,512]{1,0:T(8,128)(2,1)S(1)}, bf16[256,512]{1,0:T(8,128)(2,1)S(1)}, u32[]{:S(2)}, u32[]{:S(2)}) collective-permute-start(bf16[256,512]{1,0:T(8,128)(2,1)S(1)} %get-tuple-element.18.s0), channel_id=1, source_target_pairs={{0,16},{8,24},{16,0},{24,8},{1,17},{9,25},{17,1},{25,9},{2,18},{10... | collective-permute-start | bytes 786440 | tf_op jit(solution)/shard_map/ppermute | solution.py:264
  31.0 1.9 %collective-permute-start.2 = (bf16[256,512]{1,0:T(8,128)(2,1)S(1)}, bf16[256,512]{1,0:T(8,128)(2,1)S(1)}, u32[]{:S(2)}, u32[]{:S(2)}) collective-permute-start(bf16[256,512]{1,0:T(8,128)(2,1)S(1)} %get-tuple-element.18.s0), channel_id=1, source_target_pairs={{0,8},{8,16},{16,24},{24,0},{1,9},{9,17},{17,25},{25,1},{2,10},{10... | collective-permute-start | bytes 786440 | tf_op jit(solution)/shard_map/ppermute | solution.py:264
  32.9 4.6 %collective-permute-start.1 = (bf16[256,512]{1,0:T(8,128)(2,1)S(1)}, bf16[256,512]{1,0:T(8,128)(2,1)S(1)}, u32[]{:S(2)}, u32[]{:S(2)}) collective-permute-start(bf16[256,512]{1,0:T(8,128)(2,1)S(1)} %get-tuple-element.18.s0), channel_id=1, source_target_pairs={{0,24},{8,0},{16,8},{24,16},{1,25},{9,1},{17,9},{25,17},{2,26},{10... | collective-permute-start | bytes 786440 | tf_op jit(solution)/shard_map/ppermute | solution.py:264
  37.5 7.5 %collective-permute-start.7 = (bf16[128,1024]{1,0:T(8,128)(2,1)S(1)}, bf16[128,1024]{1,0:T(8,128)(2,1)S(1)}, u32[]{:S(2)}, u32[]{:S(2)}) collective-permute-start(bf16[128,1024]{1,0:T(8,128)(2,1)S(1)} %bitcast.1), channel_id=1, source_target_pairs={{0,448},{32,480},{64,0},{96,32},{128,64},{160,96},{192,128},{224,1... | collective-permute-start | bytes 786440 | tf_op jit(solution)/shard_map/ppermute | solution.py:264
  46.1 1.9 %collective-permute-start.6 = (bf16[128,1024]{1,0:T(8,128)(2,1)S(1)}, bf16[128,1024]{1,0:T(8,128)(2,1)S(1)}, u32[]{:S(2)}, u32[]{:S(2)}) collective-permute-start(bf16[128,1024]{1,0:T(8,128)(2,1)S(1)} %bitcast.2), channel_id=1, source_target_pairs={{0,32},{32,64},{64,96},{96,128},{128,160},{160,192},{192,224},{224... | collective-permute-start | bytes 786440 | tf_op jit(solution)/shard_map/ppermute | solution.py:264
  48.0 4.6 %collective-permute-start.5 = (bf16[128,1024]{1,0:T(8,128)(2,1)S(1)}, bf16[128,1024]{1,0:T(8,128)(2,1)S(1)}, u32[]{:S(2)}, u32[]{:S(2)}) collective-permute-start(bf16[128,1024]{1,0:T(8,128)(2,1)S(1)} %bitcast.3), channel_id=1, source_target_pairs={{0,480},{32,0},{64,32},{96,64},{128,96},{160,128},{192,160},{224,1... | collective-permute-start | bytes 786440 | tf_op jit(solution)/shard_map/ppermute | solution.py:264
  53.4 3.8 %collective-permute-start.8 = (bf16[256,512]{1,0:T(8,128)(2,1)S(1)}, bf16[256,512]{1,0:T(8,128)(2,1)S(1)}, u32[]{:S(2)}, u32[]{:S(2)}) collective-permute-start(bf16[256,512]{1,0:T(8,128)(2,1)S(1)} %get-tuple-element.19.after_ref), channel_id=1, source_target_pairs={{0,16},{8,24},{16,32},{24,40},{32,48},{40,56},{48,64},{56,72},{64,... | collective-permute-start | bytes 786440 | tf_op jit(solution)/shard_map/ppermute | solution.py:264
  57.3 4.9 %collective-permute-start.4 = (bf16[1024,512]{1,0:T(8,128)(2,1)S(1)}, bf16[1024,512]{1,0:T(8,128)(2,1)S(1)}, u32[]{:S(2)}, u32[]{:S(2)}) collective-permute-start(bf16[1024,512]{1,0:T(8,128)(2,1)S(1)} %near.1.f0), channel_id=1, source_target_pairs={{0,1},{1,0},{2,3},{3,2},{4,5},{5,4},{6,7},{7,6},{8,9},{9,8},{10,11... | collective-permute-start | bytes 3145736 | tf_op jit(solution)/shard_map/ppermute | solution.py:264
  63.0 1.5 %collective-permute-done.4.f1 = bf16[1024,512]{1,0:T(8,128)(2,1)S(1)} collective-permute-done((bf16[1024,512]{1,0:T(8,128)(2,1)S(1)}, bf16[1024,512]{1,0:T(8,128)(2,1)S(1)}, u32[]{:S(2)}, u32[]{:S(2)}) %collective-permute-start.4) | collective-permute-done | bytes 1048608 | tf_op jit(solution)/shard_map/ppermute | solution.py:264
  64.5 2.1 %project.1.parts_ref = bf16[16,288,128]{2,1,0:T(8,128)(2,1)} custom-call(bf16[1024,512]{1,0:T(8,128)(2,1)S(1)} %near.1.f0, bf16[1024,512]{1,0:T(8,128)(2,1)S(1)} %collective-permute-done.4.f1, bf16[512,1024]{1,0:T(8,128)(2,1)S(1)} %sort.1.weight_ref), custom_call_target="tpu_custom_call" | custom-call | flops 1073741824 | bytes 2097152 | tf_op jit(solution)/shard_map/project/pallas_call | solution.py:302
  66.6 3.8 %all-to-all-start.1 = ((bf16[16,288,128]{2,1,0:T(8,128)(2,1)}), bf16[16,288,128]{2,1,0:T(8,128)(2,1)S(1)}, u32[]{:S(2)}, u32[]{:S(2)}) async-start(bf16[16,288,128]{2,1,0:T(8,128)(2,1)} %gate.1.after_ref), calls=%async_computation.1 | async-start | bytes 2359296 | tf_op jit(solution)/shard_map/all_to_all | solution.py:322
  70.5 1.7 %forward.1 = (f32[256,640]{1,0:T(8,128)S(1)}, bf16[256,512]{1,0:T(8,128)(2,1)S(1)}) custom-call(f32[2]{0:T(128)S(1)} %copy-done.4, f32[264,128]{1,0:T(8,128)S(1)} %get-tuple-element.17.aux, bf16[256,512]{1,0:T(8,128)(2,1)S(1)} %copy-done, bf16[256,512]{1,0:T(8,128)(2,1)S(1)} %copy-done.1, bf16[256,512]{1,0:T(8,128)(2,1)S(1)} %copy-done.2, ...), custom_call_target="tpu_custom_call" | custom-call | flops 536870912 | bytes 2097152 | tf_op jit(solution)/shard_map/forward/pallas_call | solution.py:315
  72.2 14.7 %all-to-all-done.1.parts_ref = bf16[16,288,128]{2,1,0:T(8,128)(2,1)S(1)} async-done(((bf16[16,288,128]{2,1,0:T(8,128)(2,1)}), bf16[16,288,128]{2,1,0:T(8,128)(2,1)S(1)}, u32[]{:S(2)}, u32[]{:S(2)}) %all-to-all-start.1) | async-done | bytes 1179680 | tf_op jit(solution)/shard_map/all_to_all | solution.py:322
  88.1 4.5 %collective-permute-start.11 = (bf16[256,512]{1,0:T(8,128)(2,1)S(1)}, bf16[256,512]{1,0:T(8,128)(2,1)S(1)}, u32[]{:S(2)}, u32[]{:S(2)}) collective-permute-start(bf16[256,512]{1,0:T(8,128)(2,1)S(1)} %get-tuple-element.24), channel_id=1, source_target_pairs={{0,488},{8,496},{16,504},{24,0},{32,8},{40,16},{48,24},{56,32},{64... | collective-permute-start | bytes 786440 | tf_op jit(solution)/shard_map/ppermute | solution.py:264
  92.6 3.9 %collective-permute-start.10 = (bf16[256,512]{1,0:T(8,128)(2,1)S(1)}, bf16[256,512]{1,0:T(8,128)(2,1)S(1)}, u32[]{:S(2)}, u32[]{:S(2)}) collective-permute-start(bf16[256,512]{1,0:T(8,128)(2,1)S(1)} %get-tuple-element.24), channel_id=1, source_target_pairs={{0,496},{8,504},{16,0},{24,8},{32,16},{40,24},{48,32},{56,40},{64,... | collective-permute-start | bytes 786440 | tf_op jit(solution)/shard_map/ppermute | solution.py:264
  96.5 2.8 %collective-permute-start.9 = (bf16[256,512]{1,0:T(8,128)(2,1)S(1)}, bf16[256,512]{1,0:T(8,128)(2,1)S(1)}, u32[]{:S(2)}, u32[]{:S(2)}) collective-permute-start(bf16[256,512]{1,0:T(8,128)(2,1)S(1)} %get-tuple-element.24), channel_id=1, source_target_pairs={{0,504},{8,0},{16,8},{24,16},{32,24},{40,32},{48,40},{56,48},{64,5... | collective-permute-start | bytes 786440 | tf_op jit(solution)/shard_map/ppermute | solution.py:264
  99.4 2.0 %local.1 = (bf16[256,512]{1,0:T(8,128)(2,1)}, f32[256,512]{1,0:T(8,128)S(1)}, f32[256,512]{1,0:T(8,128)S(1)}) custom-call(f32[2]{0:T(128)S(1)} %copy-done.4, bf16[256,512]{1,0:T(8,128)(2,1)S(1)} %copy-done, bf16[256,512]{1,0:T(8,128)(2,1)S(1)} %copy-done.1, bf16[256,512]{1,0:T(8,128)(2,1)S(1)} %copy-done.2, bf16[256,512]{1,0:T(8,128)(2,1)S(1)} %get-tuple-element.21.g_ref, ...), custom_call_target="tpu_custom_call" | custom-call | flops 268435456 | bytes 2097152 | tf_op jit(solution)/shard_map/local/pallas_call | solution.py:328
  101.4 3.3 %collective-permute-done.10.s2 = bf16[256,512]{1,0:T(8,128)(2,1)S(1)} collective-permute-done((bf16[256,512]{1,0:T(8,128)(2,1)S(1)}, bf16[256,512]{1,0:T(8,128)(2,1)S(1)}, u32[]{:S(2)}, u32[]{:S(2)}) %collective-permute-start.10) | collective-permute-done | bytes 262176 | tf_op jit(solution)/shard_map/ppermute | solution.py:264
  104.7 4.9 %collective-permute-done.9.s1 = bf16[256,512]{1,0:T(8,128)(2,1)S(1)} collective-permute-done((bf16[256,512]{1,0:T(8,128)(2,1)S(1)}, bf16[256,512]{1,0:T(8,128)(2,1)S(1)}, u32[]{:S(2)}, u32[]{:S(2)}) %collective-permute-start.9) | collective-permute-done | bytes 262176 | tf_op jit(solution)/shard_map/ppermute | solution.py:264
  109.5 1.2 %final.1 = (bf16[256,512]{1,0:T(8,128)(2,1)}, bf16[256,512]{1,0:T(8,128)(2,1)}) custom-call(f32[264,128]{1,0:T(8,128)S(1)} %get-tuple-element.17.aux, bf16[256,512]{1,0:T(8,128)(2,1)S(1)} %collective-permute-done.9.s1, bf16[256,512]{1,0:T(8,128)(2,1)S(1)} %collective-permute-done.10.s2, bf16[256,512]{1,0:T(8,128)(2,1)S(1)} %collective-permute-done.11.s3, ...), custom_call_target="tpu_custom_call" | custom-call | flops 134217728 | bytes 2097152 | tf_op jit(solution)/shard_map/final/pallas_call | solution.py:331
  (27 shorter events, 4.5 us)
Async XLA Ops:
  0.6 52.0 %copy-start.4 = (f32[2]{0:T(128)S(1)}, f32[2]{0:T(128)}, u32[]{:S(2)}) copy-start(f32[2]{0:T(128)} %rate_ref.7) | copy-start | bytes 28
  0.6 52.0 %copy-start.5 = (s32[21]{0:T(128)S(1)}, s32[21]{0:T(128)}, u32[]{:S(2)}) copy-start(s32[21]{0:T(128)} %spans_ref.1) | copy-start | bytes 256
  2.2 35.2 %all-to-all-start = ((bf16[16,8,1024]{2,1,0:T(8,128)(2,1)}), bf16[16,8,1024]{2,1,0:T(8,128)(2,1)S(1)}, u32[]{:S(2)}, u32[]{:S(2)}) async-start(bf16[16,8,1024]{2,1,0:T(8,128)(2,1)} %split.1), calls=%async_computation | async-start | bytes 524288 | tf_op jit(solution)/shard_map/all_to_all | solution.py:276
  20.5 0.7 copy-start.3
  23.2 22.9 %collective-permute-start = (bf16[256,512]{1,0:T(8,128)(2,1)S(1)}, bf16[256,512]{1,0:T(8,128)(2,1)S(1)}, u32[]{:S(2)}, u32[]{:S(2)}) collective-permute-start(bf16[256,512]{1,0:T(8,128)(2,1)S(1)} %get-tuple-element.16.own), channel_id=1, source_target_pairs={{0,8},{8,16},{16,24},{24,32},{32,40},{40,48},{48,56},{56,64},{64,7... | collective-permute-start | bytes 786440 | tf_op jit(solution)/shard_map/ppermute | solution.py:264
  26.4 21.6 %collective-permute-start.3 = (bf16[256,512]{1,0:T(8,128)(2,1)S(1)}, bf16[256,512]{1,0:T(8,128)(2,1)S(1)}, u32[]{:S(2)}, u32[]{:S(2)}) collective-permute-start(bf16[256,512]{1,0:T(8,128)(2,1)S(1)} %get-tuple-element.18.s0), channel_id=1, source_target_pairs={{0,16},{8,24},{16,0},{24,8},{1,17},{9,25},{17,1},{25,9},{2,18},{10... | collective-permute-start | bytes 786440 | tf_op jit(solution)/shard_map/ppermute | solution.py:264
  31.0 22.5 %collective-permute-start.2 = (bf16[256,512]{1,0:T(8,128)(2,1)S(1)}, bf16[256,512]{1,0:T(8,128)(2,1)S(1)}, u32[]{:S(2)}, u32[]{:S(2)}) collective-permute-start(bf16[256,512]{1,0:T(8,128)(2,1)S(1)} %get-tuple-element.18.s0), channel_id=1, source_target_pairs={{0,8},{8,16},{16,24},{24,0},{1,9},{9,17},{17,25},{25,1},{2,10},{10... | collective-permute-start | bytes 786440 | tf_op jit(solution)/shard_map/ppermute | solution.py:264
  32.9 24.3 %collective-permute-start.1 = (bf16[256,512]{1,0:T(8,128)(2,1)S(1)}, bf16[256,512]{1,0:T(8,128)(2,1)S(1)}, u32[]{:S(2)}, u32[]{:S(2)}) collective-permute-start(bf16[256,512]{1,0:T(8,128)(2,1)S(1)} %get-tuple-element.18.s0), channel_id=1, source_target_pairs={{0,24},{8,0},{16,8},{24,16},{1,25},{9,1},{17,9},{25,17},{2,26},{10... | collective-permute-start | bytes 786440 | tf_op jit(solution)/shard_map/ppermute | solution.py:264
  37.5 24.7 %collective-permute-start.7 = (bf16[128,1024]{1,0:T(8,128)(2,1)S(1)}, bf16[128,1024]{1,0:T(8,128)(2,1)S(1)}, u32[]{:S(2)}, u32[]{:S(2)}) collective-permute-start(bf16[128,1024]{1,0:T(8,128)(2,1)S(1)} %bitcast.1), channel_id=1, source_target_pairs={{0,448},{32,480},{64,0},{96,32},{128,64},{160,96},{192,128},{224,1... | collective-permute-start | bytes 786440 | tf_op jit(solution)/shard_map/ppermute | solution.py:264
  46.1 16.1 %collective-permute-start.6 = (bf16[128,1024]{1,0:T(8,128)(2,1)S(1)}, bf16[128,1024]{1,0:T(8,128)(2,1)S(1)}, u32[]{:S(2)}, u32[]{:S(2)}) collective-permute-start(bf16[128,1024]{1,0:T(8,128)(2,1)S(1)} %bitcast.2), channel_id=1, source_target_pairs={{0,32},{32,64},{64,96},{96,128},{128,160},{160,192},{192,224},{224... | collective-permute-start | bytes 786440 | tf_op jit(solution)/shard_map/ppermute | solution.py:264
  48.0 14.2 %collective-permute-start.5 = (bf16[128,1024]{1,0:T(8,128)(2,1)S(1)}, bf16[128,1024]{1,0:T(8,128)(2,1)S(1)}, u32[]{:S(2)}, u32[]{:S(2)}) collective-permute-start(bf16[128,1024]{1,0:T(8,128)(2,1)S(1)} %bitcast.3), channel_id=1, source_target_pairs={{0,480},{32,0},{64,32},{96,64},{128,96},{160,128},{192,160},{224,1... | collective-permute-start | bytes 786440 | tf_op jit(solution)/shard_map/ppermute | solution.py:264
  53.4 13.1 %collective-permute-start.8 = (bf16[256,512]{1,0:T(8,128)(2,1)S(1)}, bf16[256,512]{1,0:T(8,128)(2,1)S(1)}, u32[]{:S(2)}, u32[]{:S(2)}) collective-permute-start(bf16[256,512]{1,0:T(8,128)(2,1)S(1)} %get-tuple-element.19.after_ref), channel_id=1, source_target_pairs={{0,16},{8,24},{16,32},{24,40},{32,48},{40,56},{48,64},{56,72},{64,... | collective-permute-start | bytes 786440 | tf_op jit(solution)/shard_map/ppermute | solution.py:264
  57.3 7.2 %collective-permute-start.4 = (bf16[1024,512]{1,0:T(8,128)(2,1)S(1)}, bf16[1024,512]{1,0:T(8,128)(2,1)S(1)}, u32[]{:S(2)}, u32[]{:S(2)}) collective-permute-start(bf16[1024,512]{1,0:T(8,128)(2,1)S(1)} %near.1.f0), channel_id=1, source_target_pairs={{0,1},{1,0},{2,3},{3,2},{4,5},{5,4},{6,7},{7,6},{8,9},{9,8},{10,11... | collective-permute-start | bytes 3145736 | tf_op jit(solution)/shard_map/ppermute | solution.py:264
  66.6 3.9 %copy-start = (bf16[256,512]{1,0:T(8,128)(2,1)S(1)}, bf16[256,512]{1,0:T(8,128)(2,1)}, u32[]{:S(2)}) copy-start(bf16[256,512]{1,0:T(8,128)(2,1)} %q_ref.5) | copy-start | bytes 786436
  66.6 3.9 %copy-start.1 = (bf16[256,512]{1,0:T(8,128)(2,1)S(1)}, bf16[256,512]{1,0:T(8,128)(2,1)}, u32[]{:S(2)}) copy-start(bf16[256,512]{1,0:T(8,128)(2,1)} %k_ref.5) | copy-start | bytes 786436
  66.6 3.9 %copy-start.2 = (bf16[256,512]{1,0:T(8,128)(2,1)S(1)}, bf16[256,512]{1,0:T(8,128)(2,1)}, u32[]{:S(2)}) copy-start(bf16[256,512]{1,0:T(8,128)(2,1)} %v_ref.5) | copy-start | bytes 786436
  66.6 20.3 %all-to-all-start.1 = ((bf16[16,288,128]{2,1,0:T(8,128)(2,1)}), bf16[16,288,128]{2,1,0:T(8,128)(2,1)S(1)}, u32[]{:S(2)}, u32[]{:S(2)}) async-start(bf16[16,288,128]{2,1,0:T(8,128)(2,1)} %gate.1.after_ref), calls=%async_computation.1 | async-start | bytes 2359296 | tf_op jit(solution)/shard_map/all_to_all | solution.py:322
  88.1 13.3 %collective-permute-start.11 = (bf16[256,512]{1,0:T(8,128)(2,1)S(1)}, bf16[256,512]{1,0:T(8,128)(2,1)S(1)}, u32[]{:S(2)}, u32[]{:S(2)}) collective-permute-start(bf16[256,512]{1,0:T(8,128)(2,1)S(1)} %get-tuple-element.24), channel_id=1, source_target_pairs={{0,488},{8,496},{16,504},{24,0},{32,8},{40,16},{48,24},{56,32},{64... | collective-permute-start | bytes 786440 | tf_op jit(solution)/shard_map/ppermute | solution.py:264
  92.6 12.0 %collective-permute-start.10 = (bf16[256,512]{1,0:T(8,128)(2,1)S(1)}, bf16[256,512]{1,0:T(8,128)(2,1)S(1)}, u32[]{:S(2)}, u32[]{:S(2)}) collective-permute-start(bf16[256,512]{1,0:T(8,128)(2,1)S(1)} %get-tuple-element.24), channel_id=1, source_target_pairs={{0,496},{8,504},{16,0},{24,8},{32,16},{40,24},{48,32},{56,40},{64,... | collective-permute-start | bytes 786440 | tf_op jit(solution)/shard_map/ppermute | solution.py:264
  96.5 13.0 %collective-permute-start.9 = (bf16[256,512]{1,0:T(8,128)(2,1)S(1)}, bf16[256,512]{1,0:T(8,128)(2,1)S(1)}, u32[]{:S(2)}, u32[]{:S(2)}) collective-permute-start(bf16[256,512]{1,0:T(8,128)(2,1)S(1)} %get-tuple-element.24), channel_id=1, source_target_pairs={{0,504},{8,0},{16,8},{24,16},{32,24},{40,32},{48,40},{56,48},{64,5... | collective-permute-start | bytes 786440 | tf_op jit(solution)/shard_map/ppermute | solution.py:264

commit v4 on v3

--- a/solution.py
+++ b/solution.py
@@ -15,7 +15,7 @@
 F32 = jnp.float32
 BF16 = jnp.bfloat16
 PREC = lax.Precision.HIGHEST
-NEAR = (0, 1, -1, 2)
+NEAR = (0, -1, 1, 2)
 LOW = 32
 SENT = SPAN + LOW
 

time: 112 us -> 112 us (level)
    ppermute x12, waiting for transfers between devices: 10.8 us -> 9.6 us  [shift(): return lax.ppermute(x, axes, [(i, (i + by) % size) for i in range(size)])]
    all_to_all x1, starting transfers between devices: 3.84 us -> 5.01 us  [shards(): parts = lax.all_to_all(partial, ('y', 'x'), 0, 0)]
  transfers between devices with their start and end apart: 14 -> 14, of which waited for: 5 -> 6; matrix products, arithmetic and copies ran while one was open for 0% -> 0% of each run, Pallas kernels for 9% -> 9%
where the time goes in v4:
time: 112 us; the launch traced here: 111 us
  starting transfers between devices  71.2 us (64%)
  waiting for transfers between devices  24.5 us (22%)
  Pallas kernels  13.3 us (12%)
    ppermute x12, starting transfers between devices, shift(): return lax.ppermute(x, axes, [(i, (i + by) % size) for i in range(size)])  48 us
    all_to_all x1, starting transfers between devices, shards(): held = lax.all_to_all(split, ('z1', 'x'), 0, 0).reshape(128, 1024)  18.2 us
    all_to_all x1, waiting for transfers between devices, shards(): parts = lax.all_to_all(partial, ('y', 'x'), 0, 0)  14.9 us
    ppermute x12, waiting for transfers between devices, shift(): return lax.ppermute(x, axes, [(i, (i + by) % size) for i in range(size)])  9.6 us
    all_to_all x1, starting transfers between devices, shards(): parts = lax.all_to_all(partial, ('y', 'x'), 0, 0)  5.01 us
  transfers between devices with their start and end apart: 14, of which 6 were waited for; matrix products, arithmetic and copies ran while one was open for 0% of the time, Pallas kernels for 9%

profile of v4, /device:TPU:1, one launch (start us, length us, event | category | flops | bytes accessed | tf_op | source)
XLA Modules:
  0.0 110.6 jit_solution(7234957034146055545)
XLA Ops:
  0.7 1.6 %split.1 = bf16[16,8,1024]{2,1,0:T(8,128)(2,1)} custom-call(bf16[2,4,4096]{2,1,0:T(4,128)(2,1)} %w_hbm.1), custom_call_target="tpu_custom_call" | custom-call | bytes 2097152 | tf_op jit(solution)/shard_map/split/pallas_call | solution.py:269
  2.2 18.2 %all-to-all-start = ((bf16[16,8,1024]{2,1,0:T(8,128)(2,1)}), bf16[16,8,1024]{2,1,0:T(8,128)(2,1)S(1)}, u32[]{:S(2)}, u32[]{:S(2)}) async-start(bf16[16,8,1024]{2,1,0:T(8,128)(2,1)} %split.1), calls=%async_computation | async-start | bytes 524288 | tf_op jit(solution)/shard_map/all_to_all | solution.py:276
  21.1 2.1 %update.1 = (bf16[256,512]{1,0:T(8,128)(2,1)S(1)}, bf16[256,512]{1,0:T(8,128)(2,1)S(1)}) custom-call(f32[2]{0:T(128)S(1)} %copy-done.3, bf16[256,512]{1,0:T(8,128)(2,1)} %k_ref.5, bf16[256,512]{1,0:T(8,128)(2,1)} %v_ref.5, bf16[256,512]{1,0:T(8,128)(2,1)} %feat_ref.1), custom_call_target="tpu_custom_call" | custom-call | flops 268435456 | bytes 2097152 | tf_op jit(solution)/shard_map/update/pallas_call | solution.py:277
  23.2 3.2 %collective-permute-start = (bf16[256,512]{1,0:T(8,128)(2,1)S(1)}, bf16[256,512]{1,0:T(8,128)(2,1)S(1)}, u32[]{:S(2)}, u32[]{:S(2)}) collective-permute-start(bf16[256,512]{1,0:T(8,128)(2,1)S(1)} %get-tuple-element.16.own), channel_id=1, source_target_pairs={{0,8},{8,16},{16,24},{24,32},{32,40},{40,48},{48,56},{56,64},{64,7... | collective-permute-start | bytes 786440 | tf_op jit(solution)/shard_map/ppermute | solution.py:264
  26.4 4.5 %collective-permute-start.3 = (bf16[256,512]{1,0:T(8,128)(2,1)S(1)}, bf16[256,512]{1,0:T(8,128)(2,1)S(1)}, u32[]{:S(2)}, u32[]{:S(2)}) collective-permute-start(bf16[256,512]{1,0:T(8,128)(2,1)S(1)} %get-tuple-element.18.s0), channel_id=1, source_target_pairs={{0,16},{8,24},{16,0},{24,8},{1,17},{9,25},{17,1},{25,9},{2,18},{10... | collective-permute-start | bytes 786440 | tf_op jit(solution)/shard_map/ppermute | solution.py:264
  31.0 1.9 %collective-permute-start.2 = (bf16[256,512]{1,0:T(8,128)(2,1)S(1)}, bf16[256,512]{1,0:T(8,128)(2,1)S(1)}, u32[]{:S(2)}, u32[]{:S(2)}) collective-permute-start(bf16[256,512]{1,0:T(8,128)(2,1)S(1)} %get-tuple-element.18.s0), channel_id=1, source_target_pairs={{0,8},{8,16},{16,24},{24,0},{1,9},{9,17},{17,25},{25,1},{2,10},{10... | collective-permute-start | bytes 786440 | tf_op jit(solution)/shard_map/ppermute | solution.py:264
  32.9 4.6 %collective-permute-start.1 = (bf16[256,512]{1,0:T(8,128)(2,1)S(1)}, bf16[256,512]{1,0:T(8,128)(2,1)S(1)}, u32[]{:S(2)}, u32[]{:S(2)}) collective-permute-start(bf16[256,512]{1,0:T(8,128)(2,1)S(1)} %get-tuple-element.18.s0), channel_id=1, source_target_pairs={{0,24},{8,0},{16,8},{24,16},{1,25},{9,1},{17,9},{25,17},{2,26},{10... | collective-permute-start | bytes 786440 | tf_op jit(solution)/shard_map/ppermute | solution.py:264
  37.5 7.5 %collective-permute-start.7 = (bf16[128,1024]{1,0:T(8,128)(2,1)S(1)}, bf16[128,1024]{1,0:T(8,128)(2,1)S(1)}, u32[]{:S(2)}, u32[]{:S(2)}) collective-permute-start(bf16[128,1024]{1,0:T(8,128)(2,1)S(1)} %bitcast.1), channel_id=1, source_target_pairs={{0,448},{32,480},{64,0},{96,32},{128,64},{160,96},{192,128},{224,1... | collective-permute-start | bytes 786440 | tf_op jit(solution)/shard_map/ppermute | solution.py:264
  46.1 2.5 %collective-permute-start.6 = (bf16[128,1024]{1,0:T(8,128)(2,1)S(1)}, bf16[128,1024]{1,0:T(8,128)(2,1)S(1)}, u32[]{:S(2)}, u32[]{:S(2)}) collective-permute-start(bf16[128,1024]{1,0:T(8,128)(2,1)S(1)} %bitcast.2), channel_id=1, source_target_pairs={{0,480},{32,0},{64,32},{96,64},{128,96},{160,128},{192,160},{224,1... | collective-permute-start | bytes 786440 | tf_op jit(solution)/shard_map/ppermute | solution.py:264
  48.6 2.8 %collective-permute-start.5 = (bf16[128,1024]{1,0:T(8,128)(2,1)S(1)}, bf16[128,1024]{1,0:T(8,128)(2,1)S(1)}, u32[]{:S(2)}, u32[]{:S(2)}) collective-permute-start(bf16[128,1024]{1,0:T(8,128)(2,1)S(1)} %bitcast.3), channel_id=1, source_target_pairs={{0,32},{32,64},{64,96},{96,128},{128,160},{160,192},{192,224},{224... | collective-permute-start | bytes 786440 | tf_op jit(solution)/shard_map/ppermute | solution.py:264
  52.2 3.8 %collective-permute-start.8 = (bf16[256,512]{1,0:T(8,128)(2,1)S(1)}, bf16[256,512]{1,0:T(8,128)(2,1)S(1)}, u32[]{:S(2)}, u32[]{:S(2)}) collective-permute-start(bf16[256,512]{1,0:T(8,128)(2,1)S(1)} %get-tuple-element.19.after_ref), channel_id=1, source_target_pairs={{0,16},{8,24},{16,32},{24,40},{32,48},{40,56},{48,64},{56,72},{64,... | collective-permute-start | bytes 786440 | tf_op jit(solution)/shard_map/ppermute | solution.py:264
  56.1 4.9 %collective-permute-start.4 = (bf16[1024,512]{1,0:T(8,128)(2,1)S(1)}, bf16[1024,512]{1,0:T(8,128)(2,1)S(1)}, u32[]{:S(2)}, u32[]{:S(2)}) collective-permute-start(bf16[1024,512]{1,0:T(8,128)(2,1)S(1)} %near.1.f0), channel_id=1, source_target_pairs={{0,1},{1,0},{2,3},{3,2},{4,5},{5,4},{6,7},{7,6},{8,9},{9,8},{10,11... | collective-permute-start | bytes 3145736 | tf_op jit(solution)/shard_map/ppermute | solution.py:264
  61.9 1.4 %collective-permute-done.4.f1 = bf16[1024,512]{1,0:T(8,128)(2,1)S(1)} collective-permute-done((bf16[1024,512]{1,0:T(8,128)(2,1)S(1)}, bf16[1024,512]{1,0:T(8,128)(2,1)S(1)}, u32[]{:S(2)}, u32[]{:S(2)}) %collective-permute-start.4) | collective-permute-done | bytes 1048608 | tf_op jit(solution)/shard_map/ppermute | solution.py:264
  63.3 2.1 %project.1.parts_ref = bf16[16,288,128]{2,1,0:T(8,128)(2,1)} custom-call(bf16[1024,512]{1,0:T(8,128)(2,1)S(1)} %near.1.f0, bf16[1024,512]{1,0:T(8,128)(2,1)S(1)} %collective-permute-done.4.f1, bf16[512,1024]{1,0:T(8,128)(2,1)S(1)} %sort.1.weight_ref), custom_call_target="tpu_custom_call" | custom-call | flops 1073741824 | bytes 2097152 | tf_op jit(solution)/shard_map/project/pallas_call | solution.py:302
  65.4 5.0 %all-to-all-start.1 = ((bf16[16,288,128]{2,1,0:T(8,128)(2,1)}), bf16[16,288,128]{2,1,0:T(8,128)(2,1)S(1)}, u32[]{:S(2)}, u32[]{:S(2)}) async-start(bf16[16,288,128]{2,1,0:T(8,128)(2,1)} %gate.1.after_ref), calls=%async_computation.1 | async-start | bytes 2359296 | tf_op jit(solution)/shard_map/all_to_all | solution.py:322
  70.4 1.7 %forward.1 = (f32[256,640]{1,0:T(8,128)S(1)}, bf16[256,512]{1,0:T(8,128)(2,1)S(1)}) custom-call(f32[2]{0:T(128)S(1)} %copy-done.4, f32[264,128]{1,0:T(8,128)S(1)} %get-tuple-element.17.aux, bf16[256,512]{1,0:T(8,128)(2,1)S(1)} %copy-done, bf16[256,512]{1,0:T(8,128)(2,1)S(1)} %copy-done.1, bf16[256,512]{1,0:T(8,128)(2,1)S(1)} %copy-done.2, ...), custom_call_target="tpu_custom_call" | custom-call | flops 536870912 | bytes 2097152 | tf_op jit(solution)/shard_map/forward/pallas_call | solution.py:315
  72.2 14.9 %all-to-all-done.1.parts_ref = bf16[16,288,128]{2,1,0:T(8,128)(2,1)S(1)} async-done(((bf16[16,288,128]{2,1,0:T(8,128)(2,1)}), bf16[16,288,128]{2,1,0:T(8,128)(2,1)S(1)}, u32[]{:S(2)}, u32[]{:S(2)}) %all-to-all-start.1) | async-done | bytes 1179680 | tf_op jit(solution)/shard_map/all_to_all | solution.py:322
  88.2 3.8 %collective-permute-start.11 = (bf16[256,512]{1,0:T(8,128)(2,1)S(1)}, bf16[256,512]{1,0:T(8,128)(2,1)S(1)}, u32[]{:S(2)}, u32[]{:S(2)}) collective-permute-start(bf16[256,512]{1,0:T(8,128)(2,1)S(1)} %get-tuple-element.24), channel_id=1, source_target_pairs={{0,488},{8,496},{16,504},{24,0},{32,8},{40,16},{48,24},{56,32},{64... | collective-permute-start | bytes 786440 | tf_op jit(solution)/shard_map/ppermute | solution.py:264
  92.0 5.7 %collective-permute-start.10 = (bf16[256,512]{1,0:T(8,128)(2,1)S(1)}, bf16[256,512]{1,0:T(8,128)(2,1)S(1)}, u32[]{:S(2)}, u32[]{:S(2)}) collective-permute-start(bf16[256,512]{1,0:T(8,128)(2,1)S(1)} %get-tuple-element.24), channel_id=1, source_target_pairs={{0,496},{8,504},{16,0},{24,8},{32,16},{40,24},{48,32},{56,40},{64,... | collective-permute-start | bytes 786440 | tf_op jit(solution)/shard_map/ppermute | solution.py:264
  97.7 2.8 %collective-permute-start.9 = (bf16[256,512]{1,0:T(8,128)(2,1)S(1)}, bf16[256,512]{1,0:T(8,128)(2,1)S(1)}, u32[]{:S(2)}, u32[]{:S(2)}) collective-permute-start(bf16[256,512]{1,0:T(8,128)(2,1)S(1)} %get-tuple-element.24), channel_id=1, source_target_pairs={{0,504},{8,0},{16,8},{24,16},{32,24},{40,32},{48,40},{56,48},{64,5... | collective-permute-start | bytes 786440 | tf_op jit(solution)/shard_map/ppermute | solution.py:264
  100.5 2.0 %local.1 = (bf16[256,512]{1,0:T(8,128)(2,1)}, f32[256,512]{1,0:T(8,128)S(1)}, f32[256,512]{1,0:T(8,128)S(1)}) custom-call(f32[2]{0:T(128)S(1)} %copy-done.4, bf16[256,512]{1,0:T(8,128)(2,1)S(1)} %copy-done, bf16[256,512]{1,0:T(8,128)(2,1)S(1)} %copy-done.1, bf16[256,512]{1,0:T(8,128)(2,1)S(1)} %copy-done.2, bf16[256,512]{1,0:T(8,128)(2,1)S(1)} %get-tuple-element.21.g_ref, ...), custom_call_target="tpu_custom_call" | custom-call | flops 268435456 | bytes 2097152 | tf_op jit(solution)/shard_map/local/pallas_call | solution.py:328
  102.5 2.7 %collective-permute-done.10.s2 = bf16[256,512]{1,0:T(8,128)(2,1)S(1)} collective-permute-done((bf16[256,512]{1,0:T(8,128)(2,1)S(1)}, bf16[256,512]{1,0:T(8,128)(2,1)S(1)}, u32[]{:S(2)}, u32[]{:S(2)}) %collective-permute-start.10) | collective-permute-done | bytes 262176 | tf_op jit(solution)/shard_map/ppermute | solution.py:264
  105.2 4.2 %collective-permute-done.9.s1 = bf16[256,512]{1,0:T(8,128)(2,1)S(1)} collective-permute-done((bf16[256,512]{1,0:T(8,128)(2,1)S(1)}, bf16[256,512]{1,0:T(8,128)(2,1)S(1)}, u32[]{:S(2)}, u32[]{:S(2)}) %collective-permute-start.9) | collective-permute-done | bytes 262176 | tf_op jit(solution)/shard_map/ppermute | solution.py:264
  109.5 1.2 %final.1 = (bf16[256,512]{1,0:T(8,128)(2,1)}, bf16[256,512]{1,0:T(8,128)(2,1)}) custom-call(f32[264,128]{1,0:T(8,128)S(1)} %get-tuple-element.17.aux, bf16[256,512]{1,0:T(8,128)(2,1)S(1)} %collective-permute-done.9.s1, bf16[256,512]{1,0:T(8,128)(2,1)S(1)} %collective-permute-done.10.s2, bf16[256,512]{1,0:T(8,128)(2,1)S(1)} %collective-permute-done.11.s3, ...), custom_call_target="tpu_custom_call" | custom-call | flops 134217728 | bytes 2097152 | tf_op jit(solution)/shard_map/final/pallas_call | solution.py:331
  (27 shorter events, 4.7 us)
Async XLA Ops:
  0.6 50.8 %copy-start.4 = (f32[2]{0:T(128)S(1)}, f32[2]{0:T(128)}, u32[]{:S(2)}) copy-start(f32[2]{0:T(128)} %rate_ref.7) | copy-start | bytes 28
  0.6 50.8 %copy-start.5 = (s32[21]{0:T(128)S(1)}, s32[21]{0:T(128)}, u32[]{:S(2)}) copy-start(s32[21]{0:T(128)} %spans_ref.1) | copy-start | bytes 256
  2.2 35.2 %all-to-all-start = ((bf16[16,8,1024]{2,1,0:T(8,128)(2,1)}), bf16[16,8,1024]{2,1,0:T(8,128)(2,1)S(1)}, u32[]{:S(2)}, u32[]{:S(2)}) async-start(bf16[16,8,1024]{2,1,0:T(8,128)(2,1)} %split.1), calls=%async_computation | async-start | bytes 524288 | tf_op jit(solution)/shard_map/all_to_all | solution.py:276
  20.5 0.7 copy-start.3
  23.2 22.9 %collective-permute-start = (bf16[256,512]{1,0:T(8,128)(2,1)S(1)}, bf16[256,512]{1,0:T(8,128)(2,1)S(1)}, u32[]{:S(2)}, u32[]{:S(2)}) collective-permute-start(bf16[256,512]{1,0:T(8,128)(2,1)S(1)} %get-tuple-element.16.own), channel_id=1, source_target_pairs={{0,8},{8,16},{16,24},{24,32},{32,40},{40,48},{48,56},{56,64},{64,7... | collective-permute-start | bytes 786440 | tf_op jit(solution)/shard_map/ppermute | solution.py:264
  26.4 22.2 %collective-permute-start.3 = (bf16[256,512]{1,0:T(8,128)(2,1)S(1)}, bf16[256,512]{1,0:T(8,128)(2,1)S(1)}, u32[]{:S(2)}, u32[]{:S(2)}) collective-permute-start(bf16[256,512]{1,0:T(8,128)(2,1)S(1)} %get-tuple-element.18.s0), channel_id=1, source_target_pairs={{0,16},{8,24},{16,0},{24,8},{1,17},{9,25},{17,1},{25,9},{2,18},{10... | collective-permute-start | bytes 786440 | tf_op jit(solution)/shard_map/ppermute | solution.py:264
  31.0 21.3 %collective-permute-start.2 = (bf16[256,512]{1,0:T(8,128)(2,1)S(1)}, bf16[256,512]{1,0:T(8,128)(2,1)S(1)}, u32[]{:S(2)}, u32[]{:S(2)}) collective-permute-start(bf16[256,512]{1,0:T(8,128)(2,1)S(1)} %get-tuple-element.18.s0), channel_id=1, source_target_pairs={{0,8},{8,16},{16,24},{24,0},{1,9},{9,17},{17,25},{25,1},{2,10},{10... | collective-permute-start | bytes 786440 | tf_op jit(solution)/shard_map/ppermute | solution.py:264
  32.9 23.1 %collective-permute-start.1 = (bf16[256,512]{1,0:T(8,128)(2,1)S(1)}, bf16[256,512]{1,0:T(8,128)(2,1)S(1)}, u32[]{:S(2)}, u32[]{:S(2)}) collective-permute-start(bf16[256,512]{1,0:T(8,128)(2,1)S(1)} %get-tuple-element.18.s0), channel_id=1, source_target_pairs={{0,24},{8,0},{16,8},{24,16},{1,25},{9,1},{17,9},{25,17},{2,26},{10... | collective-permute-start | bytes 786440 | tf_op jit(solution)/shard_map/ppermute | solution.py:264
  37.5 23.5 %collective-permute-start.7 = (bf16[128,1024]{1,0:T(8,128)(2,1)S(1)}, bf16[128,1024]{1,0:T(8,128)(2,1)S(1)}, u32[]{:S(2)}, u32[]{:S(2)}) collective-permute-start(bf16[128,1024]{1,0:T(8,128)(2,1)S(1)} %bitcast.1), channel_id=1, source_target_pairs={{0,448},{32,480},{64,0},{96,32},{128,64},{160,96},{192,128},{224,1... | collective-permute-start | bytes 786440 | tf_op jit(solution)/shard_map/ppermute | solution.py:264
  46.1 15.1 %collective-permute-start.6 = (bf16[128,1024]{1,0:T(8,128)(2,1)S(1)}, bf16[128,1024]{1,0:T(8,128)(2,1)S(1)}, u32[]{:S(2)}, u32[]{:S(2)}) collective-permute-start(bf16[128,1024]{1,0:T(8,128)(2,1)S(1)} %bitcast.2), channel_id=1, source_target_pairs={{0,480},{32,0},{64,32},{96,64},{128,96},{160,128},{192,160},{224,1... | collective-permute-start | bytes 786440 | tf_op jit(solution)/shard_map/ppermute | solution.py:264
  48.6 12.6 %collective-permute-start.5 = (bf16[128,1024]{1,0:T(8,128)(2,1)S(1)}, bf16[128,1024]{1,0:T(8,128)(2,1)S(1)}, u32[]{:S(2)}, u32[]{:S(2)}) collective-permute-start(bf16[128,1024]{1,0:T(8,128)(2,1)S(1)} %bitcast.3), channel_id=1, source_target_pairs={{0,32},{32,64},{64,96},{96,128},{128,160},{160,192},{192,224},{224... | collective-permute-start | bytes 786440 | tf_op jit(solution)/shard_map/ppermute | solution.py:264
  52.2 13.1 %collective-permute-start.8 = (bf16[256,512]{1,0:T(8,128)(2,1)S(1)}, bf16[256,512]{1,0:T(8,128)(2,1)S(1)}, u32[]{:S(2)}, u32[]{:S(2)}) collective-permute-start(bf16[256,512]{1,0:T(8,128)(2,1)S(1)} %get-tuple-element.19.after_ref), channel_id=1, source_target_pairs={{0,16},{8,24},{16,32},{24,40},{32,48},{40,56},{48,64},{56,72},{64,... | collective-permute-start | bytes 786440 | tf_op jit(solution)/shard_map/ppermute | solution.py:264
  56.1 7.2 %collective-permute-start.4 = (bf16[1024,512]{1,0:T(8,128)(2,1)S(1)}, bf16[1024,512]{1,0:T(8,128)(2,1)S(1)}, u32[]{:S(2)}, u32[]{:S(2)}) collective-permute-start(bf16[1024,512]{1,0:T(8,128)(2,1)S(1)} %near.1.f0), channel_id=1, source_target_pairs={{0,1},{1,0},{2,3},{3,2},{4,5},{5,4},{6,7},{7,6},{8,9},{9,8},{10,11... | collective-permute-start | bytes 3145736 | tf_op jit(solution)/shard_map/ppermute | solution.py:264
  65.4 5.1 %copy-start = (bf16[256,512]{1,0:T(8,128)(2,1)S(1)}, bf16[256,512]{1,0:T(8,128)(2,1)}, u32[]{:S(2)}) copy-start(bf16[256,512]{1,0:T(8,128)(2,1)} %q_ref.5) | copy-start | bytes 786436
  65.4 5.1 %copy-start.1 = (bf16[256,512]{1,0:T(8,128)(2,1)S(1)}, bf16[256,512]{1,0:T(8,128)(2,1)}, u32[]{:S(2)}) copy-start(bf16[256,512]{1,0:T(8,128)(2,1)} %k_ref.5) | copy-start | bytes 786436
  65.4 5.1 %copy-start.2 = (bf16[256,512]{1,0:T(8,128)(2,1)S(1)}, bf16[256,512]{1,0:T(8,128)(2,1)}, u32[]{:S(2)}) copy-start(bf16[256,512]{1,0:T(8,128)(2,1)} %v_ref.5) | copy-start | bytes 786436
  65.4 21.6 %all-to-all-start.1 = ((bf16[16,288,128]{2,1,0:T(8,128)(2,1)}), bf16[16,288,128]{2,1,0:T(8,128)(2,1)S(1)}, u32[]{:S(2)}, u32[]{:S(2)}) async-start(bf16[16,288,128]{2,1,0:T(8,128)(2,1)} %gate.1.after_ref), calls=%async_computation.1 | async-start | bytes 2359296 | tf_op jit(solution)/shard_map/all_to_all | solution.py:322
  88.2 14.3 %collective-permute-start.11 = (bf16[256,512]{1,0:T(8,128)(2,1)S(1)}, bf16[256,512]{1,0:T(8,128)(2,1)S(1)}, u32[]{:S(2)}, u32[]{:S(2)}) collective-permute-start(bf16[256,512]{1,0:T(8,128)(2,1)S(1)} %get-tuple-element.24), channel_id=1, source_target_pairs={{0,488},{8,496},{16,504},{24,0},{32,8},{40,16},{48,24},{56,32},{64... | collective-permute-start | bytes 786440 | tf_op jit(solution)/shard_map/ppermute | solution.py:264
  92.0 13.2 %collective-permute-start.10 = (bf16[256,512]{1,0:T(8,128)(2,1)S(1)}, bf16[256,512]{1,0:T(8,128)(2,1)S(1)}, u32[]{:S(2)}, u32[]{:S(2)}) collective-permute-start(bf16[256,512]{1,0:T(8,128)(2,1)S(1)} %get-tuple-element.24), channel_id=1, source_target_pairs={{0,496},{8,504},{16,0},{24,8},{32,16},{40,24},{48,32},{56,40},{64,... | collective-permute-start | bytes 786440 | tf_op jit(solution)/shard_map/ppermute | solution.py:264
  97.7 11.7 %collective-permute-start.9 = (bf16[256,512]{1,0:T(8,128)(2,1)S(1)}, bf16[256,512]{1,0:T(8,128)(2,1)S(1)}, u32[]{:S(2)}, u32[]{:S(2)}) collective-permute-start(bf16[256,512]{1,0:T(8,128)(2,1)S(1)} %get-tuple-element.24), channel_id=1, source_target_pairs={{0,504},{8,0},{16,8},{24,16},{32,24},{40,32},{48,40},{56,48},{64,5... | collective-permute-start | bytes 786440 | tf_op jit(solution)/shard_map/ppermute | solution.py:264

commit v5 on v4

--- a/solution.py
+++ b/solution.py
@@ -104,33 +104,31 @@
     return aux[:SPAN, h : h + 1], aux[:SPAN, 2 + h : 3 + h], later
 
 
-def update_kernel(rate_ref, k_hbm, v_hbm, feat_ref, u_ref, own_ref, k_ref, v_ref, sems):
-    pairs = ((k_hbm, k_ref), (v_hbm, v_ref), (feat_ref, own_ref))
-    copies = [pltpu.make_async_copy(a, b, sems.at[i]) for i, (a, b) in enumerate(pairs)]
-    for copy in copies:
-        copy.start()
-    for copy in copies:
-        copy.wait()
-    for h in range(HEADS):
-        fade = jnp.exp(-rate_ref[h] * (SPAN - offsets()))
+def update_kernel(rate_ref, k_ref, v_ref, u_ref):
+    for h in range(HEADS):
+        fade = jnp.exp(-rate_ref[:, h : h + 1] * (SPAN - offsets()))
         k, v = k_ref[:, cols(h)].astype(F32) * fade, v_ref[:, cols(h)]
         high = k.astype(BF16)
         low = (k - high.astype(F32)).astype(BF16)
         u_ref[:, cols(h)] = (tn(high, v) + tn(low, v)).astype(BF16)
 
 
-def split_kernel(w_hbm, out_ref, w_ref, sem):
-    copy = pltpu.make_async_copy(w_hbm, w_ref, sem)
-    copy.start()
-    copy.wait()
+def split_kernel(w_hbm, rate_hbm, k_hbm, v_hbm, feat_hbm, out_ref, rate_ref, k_ref, v_ref, own_ref, w_ref, sems):
+    pairs = ((w_hbm, w_ref), (rate_hbm, rate_ref), (k_hbm, k_ref), (v_hbm, v_ref), (feat_hbm, own_ref))
+    copies = [pltpu.make_async_copy(a, b, sems.at[i]) for i, (a, b) in enumerate(pairs)]
+    for copy in copies:
+        copy.start()
+    copies[0].wait()
     w = w_ref[...].astype(F32)
     rows = jnp.concatenate([w[h] for h in range(HEADS)], axis=0).astype(BF16)
     for z in range(Z1):
         for x in range(X):
             out_ref[z * X + x] = rows[:, x * 1024 : (x + 1) * 1024]
-
-
-def near_kernel(s0, s1, s3, s2, after_ref, out_ref):
+    for copy in copies[1:]:
+        copy.wait()
+
+
+def near_kernel(s0, s3, s1, s2, after_ref, out_ref):
     for i, span in enumerate((s0, s1, s2, s3)):
         out_ref[i * SPAN : (i + 1) * SPAN] = span[...]
 
@@ -266,22 +264,16 @@
 
 def shards(queries, keys, values, out_grad, out_weight, decay_rate, doc_spans):
     block = (SPAN, HEADS * 256)
-    split = call(
+    arrays = (out_weight, decay_rate.reshape(1, HEADS), keys, values, out_grad)
+    split, rate, k_near, v_near, own = call(
         split_kernel,
         "split",
-        [HBM],
-        sds((Z1 * X, 8, 1024), BF16),
-        scratch_shapes=[pltpu.VMEM(out_weight.shape, BF16), pltpu.SemaphoreType.DMA],
-    )(pltpu.with_memory_space_constraint(out_weight, pltpu.HBM))
+        [HBM] * 5,
+        [sds((Z1 * X, 8, 1024), BF16), sds((1, HEADS), F32)] + [sds(block, BF16)] * 3,
+        scratch_shapes=[pltpu.VMEM(out_weight.shape, BF16), pltpu.SemaphoreType.DMA((5,))],
+    )(*[pltpu.with_memory_space_constraint(x, pltpu.HBM) for x in arrays])
     held = lax.all_to_all(split, ("z1", "x"), 0, 0).reshape(128, 1024)
-    update, own = call(
-        update_kernel,
-        "update",
-        [SMEM] + [HBM] * 3,
-        [sds(block, BF16)] * 2,
-        flops=1 << 28,
-        scratch_shapes=[pltpu.VMEM(block, BF16), pltpu.VMEM(block, BF16), pltpu.SemaphoreType.DMA((3,))],
-    )(decay_rate, *[pltpu.with_memory_space_constraint(x, pltpu.HBM) for x in (keys, values, out_grad)])
+    update = call(update_kernel, "update", [VMEM] * 3, sds(block, BF16), flops=1 << 28)(rate, k_near, v_near)
     spans = [own] + [shift(own, "y", Y, -j) for j in range(1, Y)]
     u1 = shift(update, CTX, Z * Y, 1)
     second, aux = call(
@@ -295,7 +287,7 @@
     rows = [held] + [shift(held, DEPTH, Z, -s) for s in NEAR[1:]]
     weight = call(sort_kernel, "sort", [VMEM] * 4, sds((512, 1024), BF16), flops=1 << 34)(*rows)
     near = call(near_kernel, "near", [VMEM] * 4 + [ANY], sds((Y * SPAN, 512), BF16))(
-        spans[0], spans[1], spans[3], spans[2], second
+        spans[0], spans[3], spans[1], spans[2], second
     )
     features = [near, shift(near, "core", CORE, 1)]
 

time: 112 us -> 112 us (level)
  waiting for transfers between devices: 24.5 us -> 25.8 us
  Pallas kernels: 13.3 us -> 12.1 us
    all_to_all x1, waiting for transfers between devices: 0.01 us -> 1.81 us  [shards(): held = lax.all_to_all(split, ('z1', 'x'), 0, 0).reshape(128, 1024)]
    pallas_call x2, Pallas kernels: 3.67 us -> 2.43 us  [the longest x1 1.92 us: shards(): call(split_kernel, 'split', [HBM] * 5, [sds((Z1 * X, 8, 1024), BF16), sds...]
  transfers between devices with their start and end apart: 14 -> 14, of which waited for: 6 -> 5; matrix products, arithmetic and copies ran while one was open for 0% -> 0% of each run, Pallas kernels for 9% -> 7%
where the time goes in v5:
time: 112 us; the launch traced here: 111 us
  starting transfers between devices  72.3 us (65%)
  waiting for transfers between devices  25.8 us (23%)
  Pallas kernels  12.1 us (11%)
    ppermute x12, starting transfers between devices, shift(): return lax.ppermute(x, axes, [(i, (i + by) % size) for i in range(size)])  49 us
    all_to_all x1, starting transfers between devices, shards(): held = lax.all_to_all(split, ('z1', 'x'), 0, 0).reshape(128, 1024)  18.2 us
    all_to_all x1, waiting for transfers between devices, shards(): parts = lax.all_to_all(partial, ('y', 'x'), 0, 0)  14.9 us
    ppermute x12, waiting for transfers between devices, shift(): return lax.ppermute(x, axes, [(i, (i + by) % size) for i in range(size)])  9.15 us
    all_to_all x1, starting transfers between devices, shards(): parts = lax.all_to_all(partial, ('y', 'x'), 0, 0)  5.02 us
  transfers between devices with their start and end apart: 14, of which 5 were waited for; matrix products, arithmetic and copies ran while one was open for 0% of the time, Pallas kernels for 7%

profile of v5, /device:TPU:1, one launch (start us, length us, event | category | flops | bytes accessed | tf_op | source)
XLA Modules:
  0.0 111.1 jit_solution(4549472065688444865)
XLA Ops:
  0.7 1.9 %split.1 = (bf16[16,8,1024]{2,1,0:T(8,128)(2,1)}, f32[1,2]{1,0:T(1,128)S(1)}, bf16[256,512]{1,0:T(8,128)(2,1)S(1)}, bf16[256,512]{1,0:T(8,128)(2,1)S(1)}, bf16[256,512]{1,0:T(8,128)(2,1)S(1)}) custom-call(bf16[2,4,4096]{2,1,0:T(4,128)(2,1)} %w_hbm.1, f32[1,2]{1,0:T(1,128)} %bitcast.7, bf16[256,512]{1,0:T(8,128)(2,1)} %k_ref.5, bf16[256,512]{1,0:T(8,128)(2,1)} %v_ref.5, ...), custom_call_target="tpu_custom_call" | custom-call | bytes 2097152 | tf_op jit(solution)/shard_map/split/pallas_call | solution.py:268
  2.6 18.2 %all-to-all-start = ((bf16[16,8,1024]{2,1,0:T(8,128)(2,1)}), bf16[16,8,1024]{2,1,0:T(8,128)(2,1)S(1)}, u32[]{:S(2)}, u32[]{:S(2)}) async-start(bf16[16,8,1024]{2,1,0:T(8,128)(2,1)} %get-tuple-element.22), calls=%async_computation | async-start | bytes 524288 | tf_op jit(solution)/shard_map/all_to_all | solution.py:275
  21.3 3.2 %collective-permute-start = (bf16[256,512]{1,0:T(8,128)(2,1)S(1)}, bf16[256,512]{1,0:T(8,128)(2,1)S(1)}, u32[]{:S(2)}, u32[]{:S(2)}) collective-permute-start(bf16[256,512]{1,0:T(8,128)(2,1)S(1)} %update.1.own), channel_id=1, source_target_pairs={{0,8},{8,16},{16,24},{24,32},{32,40},{40,48},{48,56},{56,64},{64,7... | collective-permute-start | bytes 786440 | tf_op jit(solution)/shard_map/ppermute | solution.py:262
  24.5 4.5 %collective-permute-start.3 = (bf16[256,512]{1,0:T(8,128)(2,1)S(1)}, bf16[256,512]{1,0:T(8,128)(2,1)S(1)}, u32[]{:S(2)}, u32[]{:S(2)}) collective-permute-start(bf16[256,512]{1,0:T(8,128)(2,1)S(1)} %get-tuple-element.24.s0), channel_id=1, source_target_pairs={{0,16},{8,24},{16,0},{24,8},{1,17},{9,25},{17,1},{25,9},{2,18},{10... | collective-permute-start | bytes 786440 | tf_op jit(solution)/shard_map/ppermute | solution.py:262
  29.1 3.0 %collective-permute-start.2 = (bf16[256,512]{1,0:T(8,128)(2,1)S(1)}, bf16[256,512]{1,0:T(8,128)(2,1)S(1)}, u32[]{:S(2)}, u32[]{:S(2)}) collective-permute-start(bf16[256,512]{1,0:T(8,128)(2,1)S(1)} %get-tuple-element.24.s0), channel_id=1, source_target_pairs={{0,24},{8,0},{16,8},{24,16},{1,25},{9,1},{17,9},{25,17},{2,26},{10... | collective-permute-start | bytes 786440 | tf_op jit(solution)/shard_map/ppermute | solution.py:262
  32.1 2.3 %collective-permute-start.1 = (bf16[256,512]{1,0:T(8,128)(2,1)S(1)}, bf16[256,512]{1,0:T(8,128)(2,1)S(1)}, u32[]{:S(2)}, u32[]{:S(2)}) collective-permute-start(bf16[256,512]{1,0:T(8,128)(2,1)S(1)} %get-tuple-element.24.s0), channel_id=1, source_target_pairs={{0,8},{8,16},{16,24},{24,0},{1,9},{9,17},{17,25},{25,1},{2,10},{10... | collective-permute-start | bytes 786440 | tf_op jit(solution)/shard_map/ppermute | solution.py:262
  34.4 1.8 %all-to-all-done = bf16[16,8,1024]{2,1,0:T(8,128)(2,1)S(1)} async-done(((bf16[16,8,1024]{2,1,0:T(8,128)(2,1)}), bf16[16,8,1024]{2,1,0:T(8,128)(2,1)S(1)}, u32[]{:S(2)}, u32[]{:S(2)}) %all-to-all-start) | async-done | bytes 262176 | tf_op jit(solution)/shard_map/all_to_all | solution.py:275
  36.2 9.2 %collective-permute-start.7 = (bf16[128,1024]{1,0:T(8,128)(2,1)S(1)}, bf16[128,1024]{1,0:T(8,128)(2,1)S(1)}, u32[]{:S(2)}, u32[]{:S(2)}) collective-permute-start(bf16[128,1024]{1,0:T(8,128)(2,1)S(1)} %bitcast.2), channel_id=1, source_target_pairs={{0,448},{32,480},{64,0},{96,32},{128,64},{160,96},{192,128},{224,1... | collective-permute-start | bytes 786440 | tf_op jit(solution)/shard_map/ppermute | solution.py:262
  45.4 4.1 %collective-permute-start.6 = (bf16[128,1024]{1,0:T(8,128)(2,1)S(1)}, bf16[128,1024]{1,0:T(8,128)(2,1)S(1)}, u32[]{:S(2)}, u32[]{:S(2)}) collective-permute-start(bf16[128,1024]{1,0:T(8,128)(2,1)S(1)} %bitcast.3), channel_id=1, source_target_pairs={{0,480},{32,0},{64,32},{96,64},{128,96},{160,128},{192,160},{224,1... | collective-permute-start | bytes 786440 | tf_op jit(solution)/shard_map/ppermute | solution.py:262
  49.5 1.9 %collective-permute-start.5 = (bf16[128,1024]{1,0:T(8,128)(2,1)S(1)}, bf16[128,1024]{1,0:T(8,128)(2,1)S(1)}, u32[]{:S(2)}, u32[]{:S(2)}) collective-permute-start(bf16[128,1024]{1,0:T(8,128)(2,1)S(1)} %bitcast.4), channel_id=1, source_target_pairs={{0,32},{32,64},{64,96},{96,128},{128,160},{160,192},{192,224},{224... | collective-permute-start | bytes 786440 | tf_op jit(solution)/shard_map/ppermute | solution.py:262
  52.3 4.0 %collective-permute-start.8 = (bf16[256,512]{1,0:T(8,128)(2,1)S(1)}, bf16[256,512]{1,0:T(8,128)(2,1)S(1)}, u32[]{:S(2)}, u32[]{:S(2)}) collective-permute-start(bf16[256,512]{1,0:T(8,128)(2,1)S(1)} %get-tuple-element.25.after_ref), channel_id=1, source_target_pairs={{0,16},{8,24},{16,32},{24,40},{32,48},{40,56},{48,64},{56,72},{64,... | collective-permute-start | bytes 786440 | tf_op jit(solution)/shard_map/ppermute | solution.py:262
  56.4 4.9 %collective-permute-start.4 = (bf16[1024,512]{1,0:T(8,128)(2,1)S(1)}, bf16[1024,512]{1,0:T(8,128)(2,1)S(1)}, u32[]{:S(2)}, u32[]{:S(2)}) collective-permute-start(bf16[1024,512]{1,0:T(8,128)(2,1)S(1)} %near.1.f0), channel_id=1, source_target_pairs={{0,1},{1,0},{2,3},{3,2},{4,5},{5,4},{6,7},{7,6},{8,9},{9,8},{10,11... | collective-permute-start | bytes 3145736 | tf_op jit(solution)/shard_map/ppermute | solution.py:262
  62.1 1.5 %collective-permute-done.4.f1 = bf16[1024,512]{1,0:T(8,128)(2,1)S(1)} collective-permute-done((bf16[1024,512]{1,0:T(8,128)(2,1)S(1)}, bf16[1024,512]{1,0:T(8,128)(2,1)S(1)}, u32[]{:S(2)}, u32[]{:S(2)}) %collective-permute-start.4) | collective-permute-done | bytes 1048608 | tf_op jit(solution)/shard_map/ppermute | solution.py:262
  63.6 2.0 %project.1.parts_ref = bf16[16,288,128]{2,1,0:T(8,128)(2,1)} custom-call(bf16[1024,512]{1,0:T(8,128)(2,1)S(1)} %near.1.f0, bf16[1024,512]{1,0:T(8,128)(2,1)S(1)} %collective-permute-done.4.f1, bf16[512,1024]{1,0:T(8,128)(2,1)S(1)} %sort.1.weight_ref), custom_call_target="tpu_custom_call" | custom-call | flops 1073741824 | bytes 2097152 | tf_op jit(solution)/shard_map/project/pallas_call | solution.py:294
  65.7 5.0 %all-to-all-start.1 = ((bf16[16,288,128]{2,1,0:T(8,128)(2,1)}), bf16[16,288,128]{2,1,0:T(8,128)(2,1)S(1)}, u32[]{:S(2)}, u32[]{:S(2)}) async-start(bf16[16,288,128]{2,1,0:T(8,128)(2,1)} %gate.1.after_ref), calls=%async_computation.1 | async-start | bytes 2359296 | tf_op jit(solution)/shard_map/all_to_all | solution.py:314
  70.8 1.7 %forward.1 = (f32[256,640]{1,0:T(8,128)S(1)}, bf16[256,512]{1,0:T(8,128)(2,1)S(1)}) custom-call(f32[2]{0:T(128)S(1)} %copy-done.3, f32[264,128]{1,0:T(8,128)S(1)} %get-tuple-element.23.aux, bf16[256,512]{1,0:T(8,128)(2,1)S(1)} %copy-done.2, bf16[256,512]{1,0:T(8,128)(2,1)S(1)} %copy-done, bf16[256,512]{1,0:T(8,128)(2,1)S(1)} %copy-done.1, ...), custom_call_target="tpu_custom_call" | custom-call | flops 536870912 | bytes 2097152 | tf_op jit(solution)/shard_map/forward/pallas_call | solution.py:307
  72.5 14.9 %all-to-all-done.1.parts_ref = bf16[16,288,128]{2,1,0:T(8,128)(2,1)S(1)} async-done(((bf16[16,288,128]{2,1,0:T(8,128)(2,1)}), bf16[16,288,128]{2,1,0:T(8,128)(2,1)S(1)}, u32[]{:S(2)}, u32[]{:S(2)}) %all-to-all-start.1) | async-done | bytes 1179680 | tf_op jit(solution)/shard_map/all_to_all | solution.py:314
  88.5 3.8 %collective-permute-start.11 = (bf16[256,512]{1,0:T(8,128)(2,1)S(1)}, bf16[256,512]{1,0:T(8,128)(2,1)S(1)}, u32[]{:S(2)}, u32[]{:S(2)}) collective-permute-start(bf16[256,512]{1,0:T(8,128)(2,1)S(1)} %get-tuple-element.30), channel_id=1, source_target_pairs={{0,488},{8,496},{16,504},{24,0},{32,8},{40,16},{48,24},{56,32},{64... | collective-permute-start | bytes 786440 | tf_op jit(solution)/shard_map/ppermute | solution.py:262
  92.3 5.3 %collective-permute-start.10 = (bf16[256,512]{1,0:T(8,128)(2,1)S(1)}, bf16[256,512]{1,0:T(8,128)(2,1)S(1)}, u32[]{:S(2)}, u32[]{:S(2)}) collective-permute-start(bf16[256,512]{1,0:T(8,128)(2,1)S(1)} %get-tuple-element.30), channel_id=1, source_target_pairs={{0,496},{8,504},{16,0},{24,8},{32,16},{40,24},{48,32},{56,40},{64,... | collective-permute-start | bytes 786440 | tf_op jit(solution)/shard_map/ppermute | solution.py:262
  97.6 2.8 %collective-permute-start.9 = (bf16[256,512]{1,0:T(8,128)(2,1)S(1)}, bf16[256,512]{1,0:T(8,128)(2,1)S(1)}, u32[]{:S(2)}, u32[]{:S(2)}) collective-permute-start(bf16[256,512]{1,0:T(8,128)(2,1)S(1)} %get-tuple-element.30), channel_id=1, source_target_pairs={{0,504},{8,0},{16,8},{24,16},{32,24},{40,32},{48,40},{56,48},{64,5... | collective-permute-start | bytes 786440 | tf_op jit(solution)/shard_map/ppermute | solution.py:262
  100.4 2.0 %local.1 = (bf16[256,512]{1,0:T(8,128)(2,1)}, f32[256,512]{1,0:T(8,128)S(1)}, f32[256,512]{1,0:T(8,128)S(1)}) custom-call(f32[2]{0:T(128)S(1)} %copy-done.3, bf16[256,512]{1,0:T(8,128)(2,1)S(1)} %copy-done.2, bf16[256,512]{1,0:T(8,128)(2,1)S(1)} %copy-done, bf16[256,512]{1,0:T(8,128)(2,1)S(1)} %copy-done.1, bf16[256,512]{1,0:T(8,128)(2,1)S(1)} %get-tuple-element.27.g_ref, ...), custom_call_target="tpu_custom_call" | custom-call | flops 268435456 | bytes 2097152 | tf_op jit(solution)/shard_map/local/pallas_call | solution.py:320
  102.4 3.2 %collective-permute-done.10.s2 = bf16[256,512]{1,0:T(8,128)(2,1)S(1)} collective-permute-done((bf16[256,512]{1,0:T(8,128)(2,1)S(1)}, bf16[256,512]{1,0:T(8,128)(2,1)S(1)}, u32[]{:S(2)}, u32[]{:S(2)}) %collective-permute-start.10) | collective-permute-done | bytes 262176 | tf_op jit(solution)/shard_map/ppermute | solution.py:262
  105.5 4.4 %collective-permute-done.9.s1 = bf16[256,512]{1,0:T(8,128)(2,1)S(1)} collective-permute-done((bf16[256,512]{1,0:T(8,128)(2,1)S(1)}, bf16[256,512]{1,0:T(8,128)(2,1)S(1)}, u32[]{:S(2)}, u32[]{:S(2)}) %collective-permute-start.9) | collective-permute-done | bytes 262176 | tf_op jit(solution)/shard_map/ppermute | solution.py:262
  110.0 1.2 %final.1 = (bf16[256,512]{1,0:T(8,128)(2,1)}, bf16[256,512]{1,0:T(8,128)(2,1)}) custom-call(f32[264,128]{1,0:T(8,128)S(1)} %get-tuple-element.23.aux, bf16[256,512]{1,0:T(8,128)(2,1)S(1)} %collective-permute-done.9.s1, bf16[256,512]{1,0:T(8,128)(2,1)S(1)} %collective-permute-done.10.s2, bf16[256,512]{1,0:T(8,128)(2,1)S(1)} %collective-permute-done.11.s3, ...), custom_call_target="tpu_custom_call" | custom-call | flops 134217728 | bytes 2097152 | tf_op jit(solution)/shard_map/final/pallas_call | solution.py:323
  (25 shorter events, 3.3 us)
Async XLA Ops:
  0.6 50.8 %copy-start.3 = (f32[2]{0:T(128)S(1)}, f32[2]{0:T(128)}, u32[]{:S(2)}) copy-start(f32[2]{0:T(128)} %rate_ref.5) | copy-start | bytes 28
  0.6 50.8 %copy-start.4 = (s32[21]{0:T(128)S(1)}, s32[21]{0:T(128)}, u32[]{:S(2)}) copy-start(s32[21]{0:T(128)} %spans_ref.1) | copy-start | bytes 256
  2.6 33.6 %all-to-all-start = ((bf16[16,8,1024]{2,1,0:T(8,128)(2,1)}), bf16[16,8,1024]{2,1,0:T(8,128)(2,1)S(1)}, u32[]{:S(2)}, u32[]{:S(2)}) async-start(bf16[16,8,1024]{2,1,0:T(8,128)(2,1)} %get-tuple-element.22), calls=%async_computation | async-start | bytes 524288 | tf_op jit(solution)/shard_map/all_to_all | solution.py:275
  21.3 24.0 %collective-permute-start = (bf16[256,512]{1,0:T(8,128)(2,1)S(1)}, bf16[256,512]{1,0:T(8,128)(2,1)S(1)}, u32[]{:S(2)}, u32[]{:S(2)}) collective-permute-start(bf16[256,512]{1,0:T(8,128)(2,1)S(1)} %update.1.own), channel_id=1, source_target_pairs={{0,8},{8,16},{16,24},{24,32},{32,40},{40,48},{48,56},{56,64},{64,7... | collective-permute-start | bytes 786440 | tf_op jit(solution)/shard_map/ppermute | solution.py:262
  24.5 25.0 %collective-permute-start.3 = (bf16[256,512]{1,0:T(8,128)(2,1)S(1)}, bf16[256,512]{1,0:T(8,128)(2,1)S(1)}, u32[]{:S(2)}, u32[]{:S(2)}) collective-permute-start(bf16[256,512]{1,0:T(8,128)(2,1)S(1)} %get-tuple-element.24.s0), channel_id=1, source_target_pairs={{0,16},{8,24},{16,0},{24,8},{1,17},{9,25},{17,1},{25,9},{2,18},{10... | collective-permute-start | bytes 786440 | tf_op jit(solution)/shard_map/ppermute | solution.py:262
  29.1 23.2 %collective-permute-start.2 = (bf16[256,512]{1,0:T(8,128)(2,1)S(1)}, bf16[256,512]{1,0:T(8,128)(2,1)S(1)}, u32[]{:S(2)}, u32[]{:S(2)}) collective-permute-start(bf16[256,512]{1,0:T(8,128)(2,1)S(1)} %get-tuple-element.24.s0), channel_id=1, source_target_pairs={{0,24},{8,0},{16,8},{24,16},{1,25},{9,1},{17,9},{25,17},{2,26},{10... | collective-permute-start | bytes 786440 | tf_op jit(solution)/shard_map/ppermute | solution.py:262
  32.1 24.3 %collective-permute-start.1 = (bf16[256,512]{1,0:T(8,128)(2,1)S(1)}, bf16[256,512]{1,0:T(8,128)(2,1)S(1)}, u32[]{:S(2)}, u32[]{:S(2)}) collective-permute-start(bf16[256,512]{1,0:T(8,128)(2,1)S(1)} %get-tuple-element.24.s0), channel_id=1, source_target_pairs={{0,8},{8,16},{16,24},{24,0},{1,9},{9,17},{17,25},{25,1},{2,10},{10... | collective-permute-start | bytes 786440 | tf_op jit(solution)/shard_map/ppermute | solution.py:262
  36.2 25.2 %collective-permute-start.7 = (bf16[128,1024]{1,0:T(8,128)(2,1)S(1)}, bf16[128,1024]{1,0:T(8,128)(2,1)S(1)}, u32[]{:S(2)}, u32[]{:S(2)}) collective-permute-start(bf16[128,1024]{1,0:T(8,128)(2,1)S(1)} %bitcast.2), channel_id=1, source_target_pairs={{0,448},{32,480},{64,0},{96,32},{128,64},{160,96},{192,128},{224,1... | collective-permute-start | bytes 786440 | tf_op jit(solution)/shard_map/ppermute | solution.py:262
  45.4 16.0 %collective-permute-start.6 = (bf16[128,1024]{1,0:T(8,128)(2,1)S(1)}, bf16[128,1024]{1,0:T(8,128)(2,1)S(1)}, u32[]{:S(2)}, u32[]{:S(2)}) collective-permute-start(bf16[128,1024]{1,0:T(8,128)(2,1)S(1)} %bitcast.3), channel_id=1, source_target_pairs={{0,480},{32,0},{64,32},{96,64},{128,96},{160,128},{192,160},{224,1... | collective-permute-start | bytes 786440 | tf_op jit(solution)/shard_map/ppermute | solution.py:262
  49.5 11.9 %collective-permute-start.5 = (bf16[128,1024]{1,0:T(8,128)(2,1)S(1)}, bf16[128,1024]{1,0:T(8,128)(2,1)S(1)}, u32[]{:S(2)}, u32[]{:S(2)}) collective-permute-start(bf16[128,1024]{1,0:T(8,128)(2,1)S(1)} %bitcast.4), channel_id=1, source_target_pairs={{0,32},{32,64},{64,96},{96,128},{128,160},{160,192},{192,224},{224... | collective-permute-start | bytes 786440 | tf_op jit(solution)/shard_map/ppermute | solution.py:262
  52.3 13.4 %collective-permute-start.8 = (bf16[256,512]{1,0:T(8,128)(2,1)S(1)}, bf16[256,512]{1,0:T(8,128)(2,1)S(1)}, u32[]{:S(2)}, u32[]{:S(2)}) collective-permute-start(bf16[256,512]{1,0:T(8,128)(2,1)S(1)} %get-tuple-element.25.after_ref), channel_id=1, source_target_pairs={{0,16},{8,24},{16,32},{24,40},{32,48},{40,56},{48,64},{56,72},{64,... | collective-permute-start | bytes 786440 | tf_op jit(solution)/shard_map/ppermute | solution.py:262
  56.4 7.2 %collective-permute-start.4 = (bf16[1024,512]{1,0:T(8,128)(2,1)S(1)}, bf16[1024,512]{1,0:T(8,128)(2,1)S(1)}, u32[]{:S(2)}, u32[]{:S(2)}) collective-permute-start(bf16[1024,512]{1,0:T(8,128)(2,1)S(1)} %near.1.f0), channel_id=1, source_target_pairs={{0,1},{1,0},{2,3},{3,2},{4,5},{5,4},{6,7},{7,6},{8,9},{9,8},{10,11... | collective-permute-start | bytes 3145736 | tf_op jit(solution)/shard_map/ppermute | solution.py:262
  65.7 5.1 %copy-start = (bf16[256,512]{1,0:T(8,128)(2,1)S(1)}, bf16[256,512]{1,0:T(8,128)(2,1)}, u32[]{:S(2)}) copy-start(bf16[256,512]{1,0:T(8,128)(2,1)} %k_ref.5) | copy-start | bytes 786436
  65.7 5.1 %copy-start.1 = (bf16[256,512]{1,0:T(8,128)(2,1)S(1)}, bf16[256,512]{1,0:T(8,128)(2,1)}, u32[]{:S(2)}) copy-start(bf16[256,512]{1,0:T(8,128)(2,1)} %v_ref.5) | copy-start | bytes 786436
  65.7 5.1 %copy-start.2 = (bf16[256,512]{1,0:T(8,128)(2,1)S(1)}, bf16[256,512]{1,0:T(8,128)(2,1)}, u32[]{:S(2)}) copy-start(bf16[256,512]{1,0:T(8,128)(2,1)} %q_ref.5) | copy-start | bytes 786436
  65.7 21.6 %all-to-all-start.1 = ((bf16[16,288,128]{2,1,0:T(8,128)(2,1)}), bf16[16,288,128]{2,1,0:T(8,128)(2,1)S(1)}, u32[]{:S(2)}, u32[]{:S(2)}) async-start(bf16[16,288,128]{2,1,0:T(8,128)(2,1)} %gate.1.after_ref), calls=%async_computation.1 | async-start | bytes 2359296 | tf_op jit(solution)/shard_map/all_to_all | solution.py:314
  88.5 13.9 %collective-permute-start.11 = (bf16[256,512]{1,0:T(8,128)(2,1)S(1)}, bf16[256,512]{1,0:T(8,128)(2,1)S(1)}, u32[]{:S(2)}, u32[]{:S(2)}) collective-permute-start(bf16[256,512]{1,0:T(8,128)(2,1)S(1)} %get-tuple-element.30), channel_id=1, source_target_pairs={{0,488},{8,496},{16,504},{24,0},{32,8},{40,16},{48,24},{56,32},{64... | collective-permute-start | bytes 786440 | tf_op jit(solution)/shard_map/ppermute | solution.py:262
  92.3 13.2 %collective-permute-start.10 = (bf16[256,512]{1,0:T(8,128)(2,1)S(1)}, bf16[256,512]{1,0:T(8,128)(2,1)S(1)}, u32[]{:S(2)}, u32[]{:S(2)}) collective-permute-start(bf16[256,512]{1,0:T(8,128)(2,1)S(1)} %get-tuple-element.30), channel_id=1, source_target_pairs={{0,496},{8,504},{16,0},{24,8},{32,16},{40,24},{48,32},{56,40},{64,... | collective-permute-start | bytes 786440 | tf_op jit(solution)/shard_map/ppermute | solution.py:262
  97.6 12.4 %collective-permute-start.9 = (bf16[256,512]{1,0:T(8,128)(2,1)S(1)}, bf16[256,512]{1,0:T(8,128)(2,1)S(1)}, u32[]{:S(2)}, u32[]{:S(2)}) collective-permute-start(bf16[256,512]{1,0:T(8,128)(2,1)S(1)} %get-tuple-element.30), channel_id=1, source_target_pairs={{0,504},{8,0},{16,8},{24,16},{32,24},{40,32},{48,40},{56,48},{64,5... | collective-permute-start | bytes 786440 | tf_op jit(solution)/shard_map/ppermute | solution.py:262
